TPU v7x, 32 devices: a whole 2x2x4 slice. The times are simulated.
32 devices in a mesh: head: 4 (over z), sq: 8 (over y, x, core).
Axes of the slice: x: 2, y: 2, z: 4, core: 2. Of those that a mesh axis runs over, the one named last changes fastest.
Arguments:
- layer_in: bfloat16 [8192, 2048], P(('sq', 'head')), may hold values from -6 to 6
- norm1_gain: bfloat16 [2048], P('sq'), may hold values from 0.5 to 1.5
- norm1_bias: bfloat16 [2048], P('sq'), may hold values from -1.1953125 to 1.1953125
- w_query: bfloat16 [2048, 2048], P('sq', 'head'), may hold values from -0.125 to 0.125
- w_key: bfloat16 [2048, 2048], P('sq', 'head'), may hold values from -0.125 to 0.125
- w_value: bfloat16 [2048, 4096], P('sq', 'head'), may hold values from -0.125 to 0.125
- w_swish: bfloat16 [2048, 4096], P('sq', 'head'), may hold values from -0.125 to 0.125
- w_out: bfloat16 [4096, 2048], P('head', 'sq'), may hold values from -0.1875 to 0.1875
- norm2_gain: bfloat16 [2048], P('sq'), may hold values from 0.5 to 1.5
- norm2_bias: bfloat16 [2048], P('sq'), may hold values from -1.1953125 to 1.1953125
- w_gate: bfloat16 [2048, 4096], P('sq', 'head'), may hold values from -0.125 to 0.125
- w_up: bfloat16 [2048, 4096], P('sq', 'head'), may hold values from -0.125 to 0.125
- w_down: bfloat16 [4096, 2048], P('head', 'sq'), may hold values from -0.1875 to 0.1875
- cotangent: bfloat16 [8192, 2048], P(('sq', 'head')), may hold values from -6 to 6
Outputs:
- result: bfloat16 [8192, 2048], P(('sq', 'head'))
- grad_in: float32 [8192, 2048], P(('sq', 'head'))
- grad_norm1_gain: float32 [2048], P(('head', 'sq'))
- grad_norm1_bias: float32 [2048], P(('head', 'sq'))
- grad_query: float32 [2048, 2048], P('sq', 'head')
- grad_key: float32 [2048, 2048], P('sq', 'head')
- grad_value: float32 [2048, 4096], P('sq', 'head')
- grad_swish: float32 [2048, 4096], P('sq', 'head')
- grad_out: float32 [4096, 2048], P('head', 'sq')
- grad_norm2_gain: float32 [2048], P('sq')
- grad_norm2_bias: float32 [2048], P('sq')
- grad_gate: float32 [2048, 4096], P('sq', 'head')
- grad_up: float32 [2048, 4096], P('sq', 'head')
- grad_down: float32 [4096, 2048], P('head', 'sq')
All inputs are finite; a program needn't handle non-finite values.
Results may differ from a plain program's by a relative error of at most 0.025.
Values may be sent and summed in bfloat16 or wider, within the bound.
No kernel may reach another device: no remote copies, remote signals or barrier semaphores. Data moves between devices by JAX's collectives and lax.ppermute only.
A program may use at most 320 MiB of HBM per device.

v0:
```python
import jax
import jax.numpy as jnp
from jax import lax
from jax.sharding import PartitionSpec as P

KD = 256
VD = 512
SPAN = 1024


eps_layer = 1e-05
eps_group = 1e-06
highest = lax.Precision.HIGHEST


def entering(value, axis, join, neutral, backward):
    count = lax.axis_size(axis)
    place = lax.axis_index(axis)
    ahead = count - 1 - place if backward else place
    gathered = jax.tree.map(
        lambda a, kind: lax.all_gather(a.astype(kind), axis), value, (jnp.bfloat16, jnp.bfloat16)
    )
    state = jax.tree.map(lambda a, e: jnp.zeros_like(a) + jnp.asarray(e, a.dtype), value, neutral)

    def one(turn, state):
        source = count - 1 - turn if backward else turn
        return join(
            state,
            jax.tree.map(
                lambda a, own: lax.dynamic_index_in_dim(a, source, 0, False).astype(own.dtype),
                gathered,
                value,
            ),
        )

    return lax.fori_loop(0, ahead, one, state)


def layer_norm(values, weight_gain, weight_shift):
    centered = values - jnp.mean(values, axis=-1, keepdims=True)
    spread = lax.rsqrt(jnp.mean(centered * centered, axis=-1, keepdims=True) + eps_layer)
    return centered * spread * weight_gain + weight_shift


def group_norm(values):
    return values * lax.rsqrt(jnp.mean(values * values, axis=-1, keepdims=True) + eps_group)


def swish_gate(normed, pre_gate):
    return normed * jax.nn.silu(pre_gate)


def gelu_gate(pre_gate, pre_up):
    return jax.nn.gelu(pre_gate) * pre_up


def log_decay(first_head, head_count):
    head_ids = (first_head + jnp.arange(head_count)).astype(jnp.float32)
    return jnp.log(1.0 - jnp.exp2(-5.0 - head_ids))


def project(left_side, right_side):
    return jnp.dot(left_side, right_side, preferred_element_type=jnp.float32)


def outer_sum(left_side, right_side):
    return lax.dot_general(
        left_side, right_side, (((0,), (0,)), ((), ())), preferred_element_type=jnp.float32
    )


def back_project(gradient, weight):
    return lax.dot_general(
        gradient, weight, (((1,), (1,)), ((), ())), preferred_element_type=jnp.float32
    )


def combine_decay(earlier, later_part):
    return (earlier[0] * later_part[0], later_part[0][:, None, None] * earlier[1] + later_part[1])


def decay_tables(log_rate, block_len):
    position = jnp.arange(block_len).astype(jnp.float32)
    spacing = position[:, None] - position[None, :]
    causal = spacing >= 0
    decay_mat = jnp.where(
        causal[None], jnp.exp(log_rate[:, None, None] * jnp.where(causal, spacing, 0.0)[None]), 0.0
    )
    query_decay = jnp.exp(log_rate[None, :] * (position[:, None] + 1.0))
    key_decay = jnp.exp(log_rate[None, :] * (block_len - 1.0 - position[:, None]))
    return (decay_mat, query_decay, key_decay, jnp.exp(log_rate * block_len))


def retain_forward(queries, key_rows, value_rows, log_rate, block_len):
    length, head_count, key_size = queries.shape
    value_size = value_rows.shape[2]
    blocks = length // block_len
    decay_mat, query_decay, key_decay, span_decay = decay_tables(log_rate, block_len)

    def advance(carry_state, pieces):
        query_blk, key_blk, value_blk = pieces
        scores = jnp.einsum("ihd,jhd->hij", query_blk, key_blk, preferred_element_type=jnp.float32)
        mixing = (scores * decay_mat).astype(jnp.bfloat16)
        inner_sum = jnp.einsum(
            "hij,jhe->ihe", mixing, value_blk, preferred_element_type=jnp.float32
        )
        carried = query_decay[:, :, None] * jnp.einsum(
            "ihd,hde->ihe", query_blk.astype(jnp.float32), carry_state, precision=highest
        )
        update = jnp.einsum(
            "jhd,jhe->hde",
            key_blk.astype(jnp.float32) * key_decay[:, :, None],
            value_blk.astype(jnp.float32),
            precision=highest,
        )
        return (
            span_decay[:, None, None] * carry_state + update,
            (inner_sum + carried, carry_state),
        )

    start_state = jnp.zeros((head_count, key_size, value_size), jnp.float32)
    pieces = (
        queries.reshape(blocks, block_len, head_count, key_size),
        key_rows.reshape(blocks, block_len, head_count, key_size),
        value_rows.reshape(blocks, block_len, head_count, value_size),
    )
    final_state, (outputs, states) = lax.scan(advance, start_state, pieces)
    return (outputs.reshape(length, head_count, value_size), states, final_state)


def retain_backward(queries, key_rows, value_rows, grad_rows, states, log_rate, block_len):
    length, head_count, key_size = queries.shape
    value_size = value_rows.shape[2]
    blocks = length // block_len
    decay_mat, query_decay, key_decay, span_decay = decay_tables(log_rate, block_len)

    def retreat(later_grad, pieces):
        query_blk, key_blk, value_blk, grad_blk, state_blk = pieces
        scores = jnp.einsum("ihd,jhd->hij", query_blk, key_blk, preferred_element_type=jnp.float32)
        mixing = (scores * decay_mat).astype(jnp.bfloat16)
        mixing_grad = jnp.einsum(
            "ihe,jhe->hij", grad_blk, value_blk, preferred_element_type=jnp.float32
        )
        scores_grad = (mixing_grad * decay_mat).astype(jnp.bfloat16)
        grad_wide = grad_blk.astype(jnp.float32)
        key_wide = key_blk.astype(jnp.float32)
        value_wide = value_blk.astype(jnp.float32)
        query_grad = jnp.einsum(
            "hij,jhd->ihd", scores_grad, key_blk, preferred_element_type=jnp.float32
        )
        query_grad = query_grad + query_decay[:, :, None] * jnp.einsum(
            "ihe,hde->ihd", grad_wide, state_blk, precision=highest
        )
        keys_grad = jnp.einsum(
            "hij,ihd->jhd", scores_grad, query_blk, preferred_element_type=jnp.float32
        )
        keys_grad = keys_grad + key_decay[:, :, None] * jnp.einsum(
            "jhe,hde->jhd", value_wide, later_grad, precision=highest
        )
        values_grad = jnp.einsum(
            "hij,ihe->jhe", mixing, grad_blk, preferred_element_type=jnp.float32
        )
        values_grad = values_grad + key_decay[:, :, None] * jnp.einsum(
            "jhd,hde->jhe", key_wide, later_grad, precision=highest
        )
        crossed = jnp.einsum(
            "ihd,ihe->hde",
            query_blk.astype(jnp.float32) * query_decay[:, :, None],
            grad_wide,
            precision=highest,
        )
        return (
            span_decay[:, None, None] * later_grad + crossed,
            (query_grad, keys_grad, values_grad),
        )

    start_grad = jnp.zeros((head_count, key_size, value_size), jnp.float32)
    pieces = (
        queries.reshape(blocks, block_len, head_count, key_size),
        key_rows.reshape(blocks, block_len, head_count, key_size),
        value_rows.reshape(blocks, block_len, head_count, value_size),
        grad_rows.reshape(blocks, block_len, head_count, value_size),
        states,
    )
    first_grad, (query_grad, keys_grad, values_grad) = lax.scan(
        retreat, start_grad, pieces, reverse=True
    )
    return (
        query_grad.reshape(length, head_count, key_size),
        keys_grad.reshape(length, head_count, key_size),
        values_grad.reshape(length, head_count, value_size),
        first_grad,
    )


def shards(
    layer_in,
    norm1_gain,
    norm1_bias,
    w_query,
    w_key,
    w_value,
    w_swish,
    w_out,
    norm2_gain,
    norm2_bias,
    w_gate,
    w_up,
    w_down,
    cotangent,
):
    weight_set = (
        lax.all_gather(norm1_gain, "sq", axis=0, tiled=True),
        lax.all_gather(norm1_bias, "sq", axis=0, tiled=True),
        lax.all_gather(norm2_gain, "sq", axis=0, tiled=True),
        lax.all_gather(norm2_bias, "sq", axis=0, tiled=True),
        lax.all_gather(w_query, "sq", axis=0, tiled=True),
        lax.all_gather(w_key, "sq", axis=0, tiled=True),
        lax.all_gather(w_value, "sq", axis=0, tiled=True),
        lax.all_gather(w_swish, "sq", axis=0, tiled=True),
        lax.all_gather(w_out, "sq", axis=1, tiled=True),
        lax.all_gather(w_gate, "sq", axis=0, tiled=True),
        lax.all_gather(w_up, "sq", axis=0, tiled=True),
        lax.all_gather(w_down, "sq", axis=1, tiled=True),
    )
    gain_one = weight_set[0].astype(jnp.float32)
    shift_one = weight_set[1].astype(jnp.float32)
    gain_two = weight_set[2].astype(jnp.float32)
    shift_two = weight_set[3].astype(jnp.float32)
    query_cols = weight_set[4]
    key_cols = weight_set[5]
    value_cols = weight_set[6]
    swish_cols = weight_set[7]
    out_rows = weight_set[8]
    gate_cols = weight_set[9]
    up_cols = weight_set[10]
    down_rows = weight_set[11]
    key_scale = KD ** (-0.5)
    own_rows = layer_in.shape[0]
    head_index = lax.axis_index("head")
    shard_rows = (
        lax.all_gather(layer_in, "head", axis=0, tiled=True),
        lax.all_gather(cotangent, "head", axis=0, tiled=True),
    )
    inputs = shard_rows[0].astype(jnp.float32)
    cotan_low = shard_rows[1]
    length = inputs.shape[0]
    local_heads = query_cols.shape[1] // KD
    normed_low = layer_norm(inputs, gain_one, shift_one).astype(jnp.bfloat16)
    query_low = project(normed_low, query_cols).astype(jnp.bfloat16)
    key_low = (project(normed_low, key_cols) * key_scale).astype(jnp.bfloat16)
    value_low = project(normed_low, value_cols).astype(jnp.bfloat16)
    swish_pre = project(normed_low, swish_cols)
    head_query = query_low.reshape(length, local_heads, KD)
    head_key = key_low.reshape(length, local_heads, KD)
    head_value = value_low.reshape(length, local_heads, VD)
    log_rate = log_decay(head_index * local_heads, local_heads)
    local_out, states, final_state = retain_forward(
        head_query, head_key, head_value, log_rate, SPAN
    )
    factor = jnp.exp(log_rate * length)
    identity = (jnp.ones_like(factor), jnp.zeros_like(final_state))
    incoming = entering((factor, final_state), "sq", combine_decay, identity, False)[1]
    position = jnp.arange(length).astype(jnp.float32)
    reach_decay = jnp.exp(log_rate[None, :] * (position[:, None] + 1.0))
    retained = local_out + reach_decay[:, :, None] * jnp.einsum(
        "thd,hde->the", head_query.astype(jnp.float32), incoming, precision=highest
    )
    grouped = (
        group_norm(retained)
        .astype(jnp.bfloat16)
        .reshape(length, local_heads * VD)
        .astype(jnp.float32)
    )
    gated_low = swish_gate(grouped, swish_pre).astype(jnp.bfloat16)
    branch = lax.psum(project(gated_low, out_rows).astype(jnp.bfloat16), "head").astype(jnp.float32)
    hidden = inputs + branch
    second_low = layer_norm(hidden, gain_two, shift_two).astype(jnp.bfloat16)
    gate_pre = project(second_low, gate_cols)
    up_pre = project(second_low, up_cols)
    inner_low = gelu_gate(gate_pre, up_pre).astype(jnp.bfloat16)
    down_own = lax.psum_scatter(
        project(inner_low, down_rows).astype(jnp.bfloat16), "head", scatter_dimension=0, tiled=True
    ).astype(jnp.float32)
    hidden_own = lax.dynamic_slice_in_dim(hidden, head_index * own_rows, own_rows, 0)
    result = (hidden_own + down_own).astype(jnp.bfloat16)
    grad_inner = back_project(cotan_low, down_rows)
    _, gelu_back = jax.vjp(gelu_gate, gate_pre, up_pre)
    gate_grad, up_grad = gelu_back(grad_inner)
    gate_low = gate_grad.astype(jnp.bfloat16)
    up_low = up_grad.astype(jnp.bfloat16)
    second_grad = back_project(gate_low, gate_cols) + back_project(up_low, up_cols)
    _, second_back = jax.vjp(layer_norm, hidden, gain_two, shift_two)
    hidden_part, gain_two_part, shift_two_part = second_back(second_grad)
    hidden_sums = (
        lax.psum(hidden_part.astype(jnp.bfloat16), "head").astype(jnp.float32),
        lax.psum(gain_two_part.astype(jnp.bfloat16), "head").astype(jnp.float32),
        lax.psum(shift_two_part.astype(jnp.bfloat16), "head").astype(jnp.float32),
    )
    grad_hidden = cotan_low.astype(jnp.float32) + hidden_sums[0]
    branch_low = grad_hidden.astype(jnp.bfloat16)
    gated_grad = back_project(branch_low, out_rows)
    _, swish_back = jax.vjp(swish_gate, grouped, swish_pre)
    grouped_grad, swish_grad = swish_back(gated_grad)
    swish_low = swish_grad.astype(jnp.bfloat16)
    grouped_grad = (
        grouped_grad.astype(jnp.bfloat16).astype(jnp.float32).reshape(length, local_heads, VD)
    )
    _, group_back = jax.vjp(group_norm, retained)
    retained_grad = group_back(grouped_grad)[0].astype(jnp.bfloat16)
    query_grad, keys_grad, values_grad, first_grad = retain_backward(
        head_query, head_key, head_value, retained_grad, states, log_rate, SPAN
    )
    returned = entering((factor, first_grad), "sq", combine_decay, identity, True)[1]
    tail_decay = jnp.exp(log_rate[None, :] * (length - 1.0 - position[:, None]))
    query_grad = query_grad + reach_decay[:, :, None] * jnp.einsum(
        "the,hde->thd", retained_grad.astype(jnp.float32), incoming, precision=highest
    )
    keys_grad = keys_grad + tail_decay[:, :, None] * jnp.einsum(
        "the,hde->thd", head_value.astype(jnp.float32), returned, precision=highest
    )
    values_grad = values_grad + tail_decay[:, :, None] * jnp.einsum(
        "thd,hde->the", head_key.astype(jnp.float32), returned, precision=highest
    )
    query_back = query_grad.astype(jnp.bfloat16).reshape(length, local_heads * KD)
    key_back = keys_grad.astype(jnp.bfloat16).reshape(length, local_heads * KD) * key_scale
    value_back = values_grad.astype(jnp.bfloat16).reshape(length, local_heads * VD)
    refetched = (
        lax.all_gather(w_query, "sq", axis=0, tiled=True),
        lax.all_gather(w_key, "sq", axis=0, tiled=True),
        lax.all_gather(w_value, "sq", axis=0, tiled=True),
        lax.all_gather(w_swish, "sq", axis=0, tiled=True),
    )
    normed_grad = (
        back_project(query_back, refetched[0])
        + back_project(key_back, refetched[1])
        + back_project(value_back, refetched[2])
        + back_project(swish_low, refetched[3])
    )
    _, first_back = jax.vjp(layer_norm, inputs, gain_one, shift_one)
    input_part, gain_one_part, shift_one_part = first_back(normed_grad)
    input_sums = (
        lax.psum_scatter(
            input_part.astype(jnp.bfloat16), "head", scatter_dimension=0, tiled=True
        ).astype(jnp.float32),
        lax.psum_scatter(
            gain_one_part.astype(jnp.bfloat16), "head", scatter_dimension=0, tiled=True
        ).astype(jnp.float32),
        lax.psum_scatter(
            shift_one_part.astype(jnp.bfloat16), "head", scatter_dimension=0, tiled=True
        ).astype(jnp.float32),
    )
    grad_in = (
        lax.dynamic_slice_in_dim(grad_hidden, head_index * own_rows, own_rows, 0) + input_sums[0]
    )
    summed = (
        lax.psum_scatter(
            input_sums[1].astype(jnp.bfloat16), "sq", scatter_dimension=0, tiled=True
        ).astype(jnp.float32),
        lax.psum_scatter(
            input_sums[2].astype(jnp.bfloat16), "sq", scatter_dimension=0, tiled=True
        ).astype(jnp.float32),
        lax.psum_scatter(
            hidden_sums[1].astype(jnp.bfloat16), "sq", scatter_dimension=0, tiled=True
        ).astype(jnp.float32),
        lax.psum_scatter(
            hidden_sums[2].astype(jnp.bfloat16), "sq", scatter_dimension=0, tiled=True
        ).astype(jnp.float32),
        lax.psum_scatter(
            outer_sum(normed_low, query_back).astype(jnp.bfloat16),
            "sq",
            scatter_dimension=0,
            tiled=True,
        ).astype(jnp.float32),
        lax.psum_scatter(
            outer_sum(normed_low, key_back).astype(jnp.bfloat16),
            "sq",
            scatter_dimension=0,
            tiled=True,
        ).astype(jnp.float32),
        lax.psum_scatter(
            outer_sum(normed_low, value_back).astype(jnp.bfloat16),
            "sq",
            scatter_dimension=0,
            tiled=True,
        ).astype(jnp.float32),
        lax.psum_scatter(
            outer_sum(normed_low, swish_low).astype(jnp.bfloat16),
            "sq",
            scatter_dimension=0,
            tiled=True,
        ).astype(jnp.float32),
        lax.psum_scatter(
            outer_sum(gated_low, branch_low).astype(jnp.bfloat16),
            "sq",
            scatter_dimension=1,
            tiled=True,
        ).astype(jnp.float32),
        lax.psum_scatter(
            outer_sum(second_low, gate_low).astype(jnp.bfloat16),
            "sq",
            scatter_dimension=0,
            tiled=True,
        ).astype(jnp.float32),
        lax.psum_scatter(
            outer_sum(second_low, up_low).astype(jnp.bfloat16),
            "sq",
            scatter_dimension=0,
            tiled=True,
        ).astype(jnp.float32),
        lax.psum_scatter(
            outer_sum(inner_low, cotan_low).astype(jnp.bfloat16),
            "sq",
            scatter_dimension=1,
            tiled=True,
        ).astype(jnp.float32),
    )
    return (
        result,
        grad_in,
        summed[0],
        summed[1],
        summed[4],
        summed[5],
        summed[6],
        summed[7],
        summed[8],
        summed[2],
        summed[3],
        summed[9],
        summed[10],
        summed[11],
    )


def solution(mesh):
    return jax.shard_map(
        shards,
        mesh=mesh,
        in_specs=(
            P(("sq", "head"), None),
            P("sq"),
            P("sq"),
            P("sq", "head"),
            P("sq", "head"),
            P("sq", "head"),
            P("sq", "head"),
            P("head", "sq"),
            P("sq"),
            P("sq"),
            P("sq", "head"),
            P("sq", "head"),
            P("head", "sq"),
            P(("sq", "head"), None),
        ),
        out_specs=(
            P(("sq", "head"), None),
            P(("sq", "head"), None),
            P(("head", "sq")),
            P(("head", "sq")),
            P("sq", "head"),
            P("sq", "head"),
            P("sq", "head"),
            P("sq", "head"),
            P("head", "sq"),
            P("sq"),
            P("sq"),
            P("sq", "head"),
            P("sq", "head"),
            P("head", "sq"),
        ),
        check_vma=False,
    )
```

profile of v0, /device:TPU:0, one launch (start us, length us, event | category | flops | bytes accessed | tf_op | source)
XLA Modules:
  0.0 1517.3 jit_solution(1201994221053633008)
XLA Ops:
  10.8 10.3 all-gather.3
  21.8 8.8 all-gather.2
  30.7 62.3 %all-gather.20.cloned.1.call-done = bf16[1024,2048]{1,0:T(8,128)(2,1)} async-done(((bf16[256,2048]{1,0:T(8,128)(2,1)}), bf16[1024,2048]{1,0:T(8,128)(2,1)}) %all-gather.20.cloned.1.call-update) | async-done | bytes 4194320 | tf_op jit(solution)/shard_map/all_gather | solution.py:242
  101.0 20.5 %all-gather.26.cloned.1.call-done = bf16[2048,512]{1,0:T(8,128)(2,1)} async-done(((bf16[256,512]{1,0:T(8,128)(2,1)}), bf16[2048,512]{1,0:T(8,128)(2,1)}) %all-gather.26.cloned.1.call-update) | async-done | bytes 2097168 | tf_op jit(solution)/shard_map/all_gather | solution.py:218
  126.7 33.4 %all-gather.22.cloned.1.call-done = bf16[2048,1024]{1,0:T(8,128)(2,1)} async-done(((bf16[256,1024]{1,0:T(8,128)(2,1)}), bf16[2048,1024]{1,0:T(8,128)(2,1)}) %all-gather.22.cloned.1.call-update) | async-done | bytes 4194320 | tf_op jit(solution)/shard_map/all_gather | solution.py:219
  160.1 8.0 convolution_convert_fusion.10
  173.5 8.9 all-gather.4
  207.8 21.0 %all-gather.40.cloned.1.call-done = bf16[16,256,512]{2,1,0:T(8,128)(2,1)} async-done(((bf16[2,256,512]{2,1,0:T(8,128)(2,1)}), bf16[16,256,512]{2,1,0:T(8,128)(2,1)}) %all-gather.40.cloned.1.call-update) | async-done | bytes 4194320 | tf_op jit(solution)/shard_map/all_gather | solution.py:21
  238.4 28.9 %all-gather.28.cloned.1.call-done = bf16[2048,1024]{1,0:T(8,128)(2,1)} async-done(((bf16[256,1024]{1,0:T(8,128)(2,1)}), bf16[2048,1024]{1,0:T(8,128)(2,1)}) %all-gather.28.cloned.1.call-update) | async-done | bytes 4194320 | tf_op jit(solution)/shard_map/all_gather | solution.py:220
  267.3 11.4 fusion.12
  278.7 27.9 %all-gather.30.cloned.1.call-done = bf16[1024,2048]{1,0:T(8,128)(2,1)} async-done(((bf16[1024,256]{1,0:T(8,128)(2,1)}), bf16[1024,2048]{1,0:T(8,128)(2,1)}) %all-gather.30.cloned.1.call-update) | async-done | bytes 4194320 | tf_op jit(solution)/shard_map/all_gather | solution.py:221
  306.6 9.7 convolution_convert_fusion.7
  319.0 8.8 all-gather.6
  327.9 7.9 all-gather.5
  335.9 135.6 %all-reduce.12.cloned.1.call-done = bf16[1024,2048]{1,0:T(8,128)(2,1)} async-done(((bf16[1024,2048]{1,0:T(8,128)(2,1)}), bf16[1024,2048]{1,0:T(8,128)(2,1)}) %all-reduce.12.cloned.1.call-update) | async-done | bytes 4194320 | tf_op jit(solution)/shard_map/psum | solution.py:276
  483.4 25.9 %all-gather.32.cloned.1.call-done = bf16[2048,1024]{1,0:T(8,128)(2,1)} async-done(((bf16[256,1024]{1,0:T(8,128)(2,1)}), bf16[2048,1024]{1,0:T(8,128)(2,1)}) %all-gather.32.cloned.1.call-update) | async-done | bytes 4194320 | tf_op jit(solution)/shard_map/all_gather | solution.py:222
  509.3 10.1 fusion.81
  519.3 28.6 %all-gather.34.cloned.1.call-done = bf16[2048,1024]{1,0:T(8,128)(2,1)} async-done(((bf16[256,1024]{1,0:T(8,128)(2,1)}), bf16[2048,1024]{1,0:T(8,128)(2,1)}) %all-gather.34.cloned.1.call-update) | async-done | bytes 4194320 | tf_op jit(solution)/shard_map/all_gather | solution.py:223
  547.9 10.0 fusion.82
  557.9 72.4 %all-gather.38.cloned.1.call-done = bf16[1024,2048]{1,0:T(8,128)(2,1)} async-done(((bf16[256,2048]{1,0:T(8,128)(2,1)}), bf16[1024,2048]{1,0:T(8,128)(2,1)}) %all-gather.38.cloned.1.call-update) | async-done | bytes 4194320 | tf_op jit(solution)/shard_map/all_gather | solution.py:243
  630.4 37.9 %all-gather.36.cloned.1.call-done = bf16[1024,2048]{1,0:T(8,128)(2,1)} async-done(((bf16[1024,256]{1,0:T(8,128)(2,1)}), bf16[1024,2048]{1,0:T(8,128)(2,1)}) %all-gather.36.cloned.1.call-update) | async-done | bytes 4194320 | tf_op jit(solution)/shard_map/all_gather | solution.py:224
  668.2 14.3 multiply_convert_fusion.3
  682.6 6.8 fusion.83
  689.4 14.4 multiply_reduce_fusion
  703.8 9.7 fusion.79
  719.5 155.1 %all-reduce.14.cloned.1.call-done = bf16[1024,2048]{1,0:T(8,128)(2,1)} async-done(((bf16[1024,2048]{1,0:T(8,128)(2,1)}), bf16[1024,2048]{1,0:T(8,128)(2,1)}) %all-reduce.14.cloned.1.call-update) | async-done | bytes 4194320 | tf_op jit(solution)/shard_map/psum | solution.py:296
  874.6 13.0 fusion.23
  893.6 9.4 convolution_convert_fusion.2
  903.1 9.4 convolution_convert_fusion.1
  913.0 10.0 convolution_convert_fusion
  939.4 10.1 convolution_convert_fusion.6
  949.6 9.4 convolution_convert_fusion.4
  959.3 10.8 convolution_convert_fusion.3
  977.8 14.4 while.17
  1018.9 7.4 fusion.85
  1033.2 6.8 fusion.88
  1040.0 13.5 fusion.8
  1065.5 8.7 convert_add_fusion.3
  1078.4 14.8 reduce-scatter.29.cloned.1.call-done
  1095.4 42.7 %reduce-scatter.15.cloned.1.call-done = bf16[256,512]{1,0:T(8,128)(2,1)} async-done(((bf16[2048,512]{1,0:T(8,128)(2,1)}), bf16[256,512]{1,0:T(8,128)(2,1)}) %reduce-scatter.15.cloned.1.call-update) | async-done | bytes 262160 | tf_op jit(solution)/shard_map/reduce_scatter | solution.py:369
  1139.8 77.3 %reduce-scatter.11.cloned.1.call-done = bf16[256,2048]{1,0:T(8,128)(2,1)} async-done(((bf16[1024,2048]{1,0:T(8,128)(2,1)}), bf16[256,2048]{1,0:T(8,128)(2,1)}) %reduce-scatter.11.cloned.1.call-update) | async-done | bytes 1048592 | tf_op jit(solution)/shard_map/reduce_scatter | solution.py:282
  1220.3 52.3 %reduce-scatter.21.cloned.1.call-done = bf16[256,1024]{1,0:T(8,128)(2,1)} async-done(((bf16[2048,1024]{1,0:T(8,128)(2,1)}), bf16[256,1024]{1,0:T(8,128)(2,1)}) %reduce-scatter.21.cloned.1.call-update) | async-done | bytes 524304 | tf_op jit(solution)/shard_map/reduce_scatter | solution.py:387
  1274.7 52.6 %reduce-scatter.23.cloned.1.call-done = bf16[1024,256]{1,0:T(8,128)(2,1)} async-done(((bf16[1024,2048]{1,0:T(8,128)(2,1)}), bf16[1024,256]{1,0:T(8,128)(2,1)}) %reduce-scatter.23.cloned.1.call-update) | async-done | bytes 524304 | tf_op jit(solution)/shard_map/reduce_scatter | solution.py:393
  1329.4 11.9 all-reduce.8
  1341.4 22.5 %all-reduce.6 = (bf16[512]{0:T(512)(128)(2,1)S(1)}, bf16[512]{0:T(512)(128)(2,1)S(1)}, bf16[2048]{0:T(1024)(128)(2,1)S(1)}, bf16[2048]{0:T(1024)(128)(2,1)S(1)}) all-reduce(bf16[512]{0:T(512)(128)(2,1)S(1)} %dynamic-slice.2, bf16[512]{0:T(512)(128)(2,1)S(1)} %dynamic-slice.6, ...), channel_id=7, replica_groups=mesh['head'=4,'sq'=8] {'sq'}, use_global_device_ids=true, to_apply=%region_20.21.clone | all-reduce | flops 5120 | bytes 20480
  1364.1 8.3 all-reduce.7
  1376.5 51.0 %reduce-scatter.19.cloned.1.call-done = bf16[256,1024]{1,0:T(8,128)(2,1)} async-done(((bf16[2048,1024]{1,0:T(8,128)(2,1)}), bf16[256,1024]{1,0:T(8,128)(2,1)}) %reduce-scatter.19.cloned.1.call-update) | async-done | bytes 524304 | tf_op jit(solution)/shard_map/reduce_scatter | solution.py:381
  1429.7 76.9 %reduce-scatter.13.cloned.1.call-done = bf16[256,2048]{1,0:T(8,128)(2,1)} async-done(((bf16[1024,2048]{1,0:T(8,128)(2,1)}), bf16[256,2048]{1,0:T(8,128)(2,1)}) %reduce-scatter.13.cloned.1.call-update) | async-done | bytes 1048592 | tf_op jit(solution)/shard_map/reduce_scatter | solution.py:343
  (268 shorter events, 192.0 us)
Async XLA Ops:
  7.2 85.9 %all-gather.20.cloned.1.call-start = ((), (), s32[]{:S(2)}) async-start(), calls=%async_computation.10 | async-start | bytes 5242880 | tf_op jit(solution)/shard_map/all_gather | solution.py:242
  7.9 113.5 %all-gather.26.cloned.1.call-start = ((), (), s32[]{:S(2)}) async-start(), calls=%async_computation.13 | async-start | bytes 2359296 | tf_op jit(solution)/shard_map/all_gather | solution.py:218
  8.7 151.4 %all-gather.22.cloned.1.call-start = ((), (), s32[]{:S(2)}) async-start(), calls=%async_computation.11 | async-start | bytes 4718592 | tf_op jit(solution)/shard_map/all_gather | solution.py:219
  9.4 180.3 %all-gather.24.cloned.1.call-start = ((), (), s32[]{:S(2)}) async-start(), calls=%async_computation.12 | async-start | bytes 2359296 | tf_op jit(solution)/shard_map/all_gather | solution.py:217
  10.0 218.8 %all-gather.40.cloned.1.call-start = ((), (), s32[]{:S(2)}) async-start(), calls=%async_computation.32 | async-start | bytes 4718592 | tf_op jit(solution)/shard_map/all_gather | solution.py:21
  10.1 188.8 %copy-start.45 = (f32[2]{0:T(128)}, f32[2]{0:T(128)S(1)}, u32[]{:S(2)}) copy-start(f32[2]{0:T(128)S(1)} %subtract_log_fusion) | copy-start | bytes 28
  30.6 67.2 %copy-start.32 = (f32[8,1,256]{2,1,0:T(1,128)}, f32[8,1,256]{2,1,0:T(1,128)S(1)}, u32[]{:S(2)}) copy-start(f32[8,1,256]{2,1,0:T(1,128)S(1)} %convert_element_type.394) | copy-start | bytes 24580
  30.7 137.4 %copy-start.36 = (f32[1024,2]{0,1:T(2,128)}, f32[1024,2]{0,1:T(2,128)S(1)}, u32[]{:S(2)}) copy-start(f32[1024,2]{0,1:T(2,128)S(1)} %get-tuple-element.284) | copy-start | bytes 24580
  126.7 72.2 %copy-start.12 = (bf16[1024,512]{0,1:T(8,128)(2,1)}, bf16[1024,512]{0,1:T(8,128)(2,1)S(1)}, u32[]{:S(2)}) copy-start(bf16[1024,512]{0,1:T(8,128)(2,1)S(1)} %multiply_convert_fusion.6) | copy-start | bytes 3145732
  172.1 95.2 %all-gather.28.cloned.1.call-start = ((), (), s32[]{:S(2)}) async-start(), calls=%async_computation.14 | async-start | bytes 4718592 | tf_op jit(solution)/shard_map/all_gather | solution.py:220
  172.7 134.0 %all-gather.30.cloned.1.call-start = ((), (), s32[]{:S(2)}) async-start(), calls=%async_computation.15 | async-start | bytes 4718592 | tf_op jit(solution)/shard_map/all_gather | solution.py:221
  173.4 298.0 %all-reduce.12.cloned.1.call-start = ((), (), s32[]{:S(2)}) async-start(), calls=%async_computation.16 | async-start | bytes 8388608 | tf_op jit(solution)/shard_map/psum | solution.py:276
  183.4 15.5 %copy-start.30 = (pred[1024,1024]{1,0:T(8,128)(4,1)}, pred[1024,1024]{1,0:T(8,128)(4,1)S(1)}, u32[]{:S(2)}) copy-start(pred[1024,1024]{1,0:T(8,128)(4,1)S(1)} %subtract_compare_fusion) | copy-start | bytes 3145732
  195.0 34.4 %copy-start.15 = (bf16[1024,512]{0,1:T(8,128)(2,1)}, bf16[1024,512]{0,1:T(8,128)(2,1)S(1)}, u32[]{:S(2)}) copy-start(bf16[1024,512]{0,1:T(8,128)(2,1)S(1)} %convolution_convert_fusion.11) | copy-start | bytes 3145732
  316.3 11.6 copy-start.51
  316.3 192.9 %all-gather.32.cloned.1.call-start = ((), (), s32[]{:S(2)}) async-start(), calls=%async_computation.17 | async-start | bytes 4718592 | tf_op jit(solution)/shard_map/all_gather | solution.py:222
  317.1 230.8 %all-gather.34.cloned.1.call-start = ((), (), s32[]{:S(2)}) async-start(), calls=%async_computation.18 | async-start | bytes 4718592 | tf_op jit(solution)/shard_map/all_gather | solution.py:223
  317.6 312.7 %all-gather.38.cloned.1.call-start = ((), (), s32[]{:S(2)}) async-start(), calls=%async_computation.21 | async-start | bytes 5242880 | tf_op jit(solution)/shard_map/all_gather | solution.py:243
  318.4 349.9 %all-gather.36.cloned.1.call-start = ((), (), s32[]{:S(2)}) async-start(), calls=%async_computation.19 | async-start | bytes 4718592 | tf_op jit(solution)/shard_map/all_gather | solution.py:224
  319.0 555.6 %all-reduce.14.cloned.1.call-start = ((), (), s32[]{:S(2)}) async-start(), calls=%async_computation.22 | async-start | bytes 8388608 | tf_op jit(solution)/shard_map/psum | solution.py:296
  668.2 14.3 copy-start.49
  682.6 6.8 copy-start.57
  682.6 6.8 copy-start.2
  719.4 258.3 %all-gather.42.cloned.1.call-start = ((), (), s32[]{:S(2)}) async-start(), calls=%async_computation.33 | async-start | bytes 4718592 | tf_op jit(solution)/shard_map/all_gather | solution.py:21
  874.6 13.0 copy-start.9
  874.6 13.0 copy-start.20
  893.3 180.9 %reduce-scatter.25.cloned.1.call-start = ((), (), s32[]{:S(2)}) async-start(), calls=%async_computation.29 | async-start | bytes 4718592 | tf_op jit(solution)/shard_map/reduce_scatter | solution.py:399
  903.0 173.3 %reduce-scatter.27.cloned.1.call-start = ((), (), s32[]{:S(2)}) async-start(), calls=%async_computation.30 | async-start | bytes 4718592 | tf_op jit(solution)/shard_map/reduce_scatter | solution.py:405
  912.5 180.7 %reduce-scatter.29.cloned.1.call-start = ((), (), s32[]{:S(2)}) async-start(), calls=%async_computation.31 | async-start | bytes 4718592 | tf_op jit(solution)/shard_map/reduce_scatter | solution.py:411
  923.0 215.0 %reduce-scatter.15.cloned.1.call-start = ((), (), s32[]{:S(2)}) async-start(), calls=%async_computation.24 | async-start | bytes 2359296 | tf_op jit(solution)/shard_map/reduce_scatter | solution.py:369
  939.2 277.9 %reduce-scatter.11.cloned.1.call-start = ((), (), s32[]{:S(2)}) async-start(), calls=%async_computation.20 | async-start | bytes 5242880 | tf_op jit(solution)/shard_map/reduce_scatter | solution.py:282
  949.6 323.0 %reduce-scatter.21.cloned.1.call-start = ((), (), s32[]{:S(2)}) async-start(), calls=%async_computation.27 | async-start | bytes 4718592 | tf_op jit(solution)/shard_map/reduce_scatter | solution.py:387
  959.1 368.2 %reduce-scatter.23.cloned.1.call-start = ((), (), s32[]{:S(2)}) async-start(), calls=%async_computation.28 | async-start | bytes 4718592 | tf_op jit(solution)/shard_map/reduce_scatter | solution.py:393
  970.2 404.5 %reduce-scatter.17.cloned.1.call-start = ((), (), s32[]{:S(2)}) async-start(), calls=%async_computation.25 | async-start | bytes 2359296 | tf_op jit(solution)/shard_map/reduce_scatter | solution.py:375
  977.8 14.5 copy-start.37
  1002.4 425.2 %reduce-scatter.19.cloned.1.call-start = ((), (), s32[]{:S(2)}) async-start(), calls=%async_computation.26 | async-start | bytes 4718592 | tf_op jit(solution)/shard_map/reduce_scatter | solution.py:381
  1017.7 488.9 %reduce-scatter.13.cloned.1.call-start = ((), (), s32[]{:S(2)}) async-start(), calls=%async_computation.23 | async-start | bytes 5242880 | tf_op jit(solution)/shard_map/reduce_scatter | solution.py:343
  1018.9 7.4 copy-start.48
  1018.9 7.4 copy-start.56
  1033.1 6.9 copy-start.3
  1033.1 6.9 copy-start.22
  1033.1 6.9 copy-start.27
  1033.1 6.9 copy-start.33
  1033.1 6.9 copy-start.35
  1033.2 6.9 copy-start.39
  1040.0 13.5 copy-start.41
  1095.4 246.0 %copy-start.42 = (bf16[2048]{0:T(1024)(128)(2,1)S(1)}, bf16[2048]{0:T(1024)(128)(2,1)}, u32[]{:S(2)}) copy-start(bf16[2048]{0:T(1024)(128)(2,1)} %get-tuple-element.239) | copy-start | bytes 12292
  1095.4 246.0 %copy-start.43 = (bf16[2048]{0:T(1024)(128)(2,1)S(1)}, bf16[2048]{0:T(1024)(128)(2,1)}, u32[]{:S(2)}) copy-start(bf16[2048]{0:T(1024)(128)(2,1)} %get-tuple-element.243) | copy-start | bytes 12292
  (34 other events, 113.8 us)
Sparse Core Ops, SparseCore 0:
  9.6 83.4 all-gather.19
  95.0 26.4 all-gather.25
  123.3 36.7 all-gather.21
  161.8 27.8 all-gather.23
  192.0 36.7 all-gather.39
  230.5 36.7 all-gather.27
  269.2 37.4 all-gather.29
  316.4 154.9 all-reduce.11
  473.5 35.7 all-gather.31
  511.1 36.7 all-gather.33
  549.6 80.7 all-gather.37
  632.2 35.9 all-gather.35
  719.6 154.9 all-reduce.13
  893.4 35.7 all-gather.41
  932.4 51.3 reduce-scatter.24
  987.4 51.3 reduce-scatter.26
  1041.9 51.3 reduce-scatter.28
  1096.8 41.2 reduce-scatter.14
  1140.3 76.7 reduce-scatter.10
  1220.7 51.8 reduce-scatter.20
  1275.9 51.3 reduce-scatter.22
  1331.5 41.3 reduce-scatter.16
  1376.2 51.2 reduce-scatter.18
  1429.8 76.7 reduce-scatter.12
where the time goes:
time: 1530 us; the launch traced here: 1520 us
  waiting for transfers between devices  1030 us (67%)
  matrix products  270 us (18%)
  other arithmetic  96.9 us (6%)
  blocking collectives  87.6 us (6%)
  between operations  17.4 us (1%)
    psum x1, waiting for transfers between devices, shards(): lax.psum(hidden_part.astype(jnp.bfloat16), 'head').astype(jnp.float32)  155 us
    psum x1, waiting for transfers between devices, shards(): lax.psum(project(gated_low, out_rows).astype(jnp.bfloat16), 'head')  136 us
    dot_general x8, matrix products, back_project(): lax.dot_general(gradient, weight, (((1,), (1,)), ((), ())), preferred_ele...  83 us
    reduce_scatter x1, waiting for transfers between devices, shards(): lax.psum_scatter(project(inner_low, down_rows).astype(jnp.bfloat16), 'hea...  77.3 us
    reduce_scatter x1, waiting for transfers between devices, shards(): lax.psum_scatter(input_part.astype(jnp.bfloat16), 'head', scatter_dimensi...  76.9 us
    all_gather x1, waiting for transfers between devices, shards(): lax.all_gather(cotangent, 'head', axis=0, tiled=True)  72.4 us
    dot_general x8, matrix products, project(): return jnp.dot(left_side, right_side, preferred_element_type=jnp.float32)  69.8 us
    dot_general x8, matrix products, outer_sum(): lax.dot_general(left_side, right_side, (((0,), (0,)), ((), ())), preferre...  63.1 us
  transfers between devices with their start and end apart: 24, of which 20 were waited for; matrix products, arithmetic and copies ran while one was open for 19% of the time, Pallas kernels for 0%

commit v1 on v0

v1 whole, which is shorter than its diff:
```python
import jax
import jax.numpy as jnp
from jax import lax
from jax.sharding import PartitionSpec as P

KD = 256
VD = 512
CHUNK = 256


eps_layer = 1e-05
eps_group = 1e-06
low = jnp.bfloat16
wide = jnp.float32


def mask_of(slot, count):
    bits = count.bit_length() - 1
    return ((slot << 1) & (count - 1)) | (slot >> (bits - 1))


def slot_of(mask, count):
    bits = count.bit_length() - 1
    return (mask >> 1) | ((mask & 1) << (bits - 1))


def flip(value, mask):
    count = lax.axis_size("sq")
    return lax.ppermute(value, "sq", [(i, i ^ mask) for i in range(count)])


def route(swapped):
    count = lax.axis_size("sq")
    lower = list(range(count.bit_length() - 2))
    return lower[::-1] if swapped else lower


def own_order(values):
    count = lax.axis_size("sq")
    width = values.shape[-1] // count
    place = lax.axis_index("sq")
    return jnp.concatenate(
        [
            lax.dynamic_slice_in_dim(values, (place ^ mask_of(s, count)) * width, width, -1)
            for s in range(count)
        ],
        axis=-1,
    )


def true_order(values):
    count = lax.axis_size("sq")
    width = values.shape[-1] // count
    place = lax.axis_index("sq")
    return jnp.concatenate(
        [
            lax.dynamic_slice_in_dim(values, slot_of(place ^ b, count) * width, width, -1)
            for b in range(count)
        ],
        axis=-1,
    )


def gather_sq(shard, axis, swapped):
    count = lax.axis_size("sq")
    pieces = {0: shard}
    for bit in route(swapped):
        got = {s | 1 << bit: flip(p, mask_of(1 << bit, count)) for s, p in pieces.items()}
        pieces.update(got)
    near = jnp.concatenate([pieces[s] for s in range(count // 2)], axis=axis)
    far = flip(near, mask_of(count // 2, count))
    return jnp.concatenate([near, far], axis=axis)


def scatter_sq(product, axis, swapped):
    count = lax.axis_size("sq")
    got = flip(product(1).astype(low), mask_of(count // 2, count))
    total = (product(0) + got.astype(wide)).astype(low)
    width = total.shape[axis] // (count // 2)
    pieces = {
        s: lax.slice_in_dim(total, s * width, (s + 1) * width, axis=axis) for s in range(count // 2)
    }
    bits = route(swapped)[::-1]
    for step, bit in enumerate(bits):
        keep = [s for s in pieces if not s >> bit & 1]
        sent = jnp.concatenate([pieces[s | 1 << bit] for s in keep], axis=axis)
        got = flip(sent, mask_of(1 << bit, count)).astype(wide)
        parts = {}
        for k, s in enumerate(keep):
            part = pieces[s].astype(wide) + lax.slice_in_dim(
                got, k * width, (k + 1) * width, axis=axis
            )
            parts[s] = part if step == len(bits) - 1 else part.astype(low)
        pieces = parts
    return pieces[0]


def ring_step(value):
    count = lax.axis_size("head")
    return lax.ppermute(value, "head", [(i, (i + 1) % count) for i in range(count)])


def gather_head(rows):
    count = lax.axis_size("head")
    place = lax.axis_index("head")
    size = rows.shape[0]
    whole = jnp.zeros((count * size,) + rows.shape[1:], rows.dtype)
    held = rows
    for turn in range(count):
        whole = lax.dynamic_update_slice_in_dim(
            whole, held, lax.rem(place - turn + count, count) * size, 0
        )
        if turn < count - 1:
            held = ring_step(held)
    return whole


def scatter_head(product, size):
    count = lax.axis_size("head")
    place = lax.axis_index("head")
    total = product(lax.rem(place - 1 + count, count) * size)
    for turn in range(2, count + 1):
        got = ring_step(total.astype(low)).astype(wide)
        total = product(lax.rem(place - turn + count, count) * size) + got
    return total


def sum_all(values):
    for axis in ("sq", "head"):
        count = lax.axis_size(axis)
        step = 1
        while step < count:
            values = values + lax.ppermute(values, axis, [(i, i ^ step) for i in range(count)])
            step *= 2
    return values


def layer_norm(values, weight_gain, weight_shift):
    centered = values - jnp.mean(values, axis=-1, keepdims=True)
    spread = lax.rsqrt(jnp.mean(centered * centered, axis=-1, keepdims=True) + eps_layer)
    return centered * spread * weight_gain + weight_shift


def group_norm(values):
    return values * lax.rsqrt(jnp.mean(values * values, axis=-1, keepdims=True) + eps_group)


def swish_gate(normed, pre_gate):
    return normed * jax.nn.silu(pre_gate)


def gelu_gate(pre_gate, pre_up):
    return jax.nn.gelu(pre_gate) * pre_up


def log_decay(first_head, head_count):
    head_ids = (first_head + jnp.arange(head_count)).astype(jnp.float32)
    return jnp.log(1.0 - jnp.exp2(-5.0 - head_ids))


def project(left_side, right_side):
    return jnp.dot(left_side, right_side, preferred_element_type=jnp.float32)


def outer_sum(left_side, right_side):
    return lax.dot_general(
        left_side, right_side, (((0,), (0,)), ((), ())), preferred_element_type=jnp.float32
    )


def back_project(gradient, weight):
    return lax.dot_general(
        gradient, weight, (((1,), (1,)), ((), ())), preferred_element_type=jnp.float32
    )


def carried_from(state, log_rate, length, backward):
    count = lax.axis_size("sq")
    place = lax.axis_index("sq")
    sent = state.astype(low)
    slots = gather_sq(sent[None], 0, False)
    total = jnp.zeros_like(state)
    for slot in range(1, count):
        other = place ^ mask_of(slot, count)
        ahead = (other - place) if backward else (place - other)
        between = jnp.maximum(ahead - 1, 0).astype(wide) * length
        factor = jnp.where(ahead > 0, jnp.exp(log_rate * between), 0.0)
        total = total + factor[:, None, None] * slots[slot].astype(wide)
    return total


def heads_of(values, size):
    return values.reshape(values.shape[0], -1, size).transpose(1, 0, 2)


def rows_of(values):
    return values.transpose(1, 0, 2).reshape(values.shape[1], -1)


def retain_forward(queries, key_rows, value_rows, incoming, log_rate):
    heads, length, _ = queries.shape
    position = jnp.arange(length).astype(wide)
    spacing = position[:, None] - position[None, :]
    decay = jnp.where(
        spacing >= 0, jnp.exp(log_rate[:, None, None] * jnp.maximum(spacing, 0.0)[None]), 0.0
    )
    reach = jnp.exp(log_rate[:, None] * (position + 1.0))
    scores = jnp.einsum("hid,hjd->hij", queries, key_rows, preferred_element_type=wide)
    mixing = (scores * decay).astype(low)
    inner = jnp.einsum("hij,hje->hie", mixing, value_rows, preferred_element_type=wide)
    carried = jnp.einsum(
        "hid,hde->hie", queries, incoming.astype(low), preferred_element_type=wide
    )
    return inner + reach[:, :, None] * carried, mixing, decay


def shards(
    layer_in,
    norm1_gain,
    norm1_bias,
    w_query,
    w_key,
    w_value,
    w_swish,
    w_out,
    norm2_gain,
    norm2_bias,
    w_gate,
    w_up,
    w_down,
    cotangent,
):
    count_sq = lax.axis_size("sq")
    count_head = lax.axis_size("head")
    sq_index = lax.axis_index("sq")
    head_index = lax.axis_index("head")
    own_rows = layer_in.shape[0]
    length = own_rows * count_head
    key_scale = KD ** (-0.5)
    query_width = w_query.shape[1]
    value_width = w_value.shape[1]
    local_heads = query_width // KD

    x_own = own_order(layer_in)
    cot_own = own_order(cotangent)
    x_low = gather_head(x_own)
    norms = gather_sq(jnp.stack([norm1_gain, norm1_bias, norm2_gain, norm2_bias]), 1, False).astype(
        wide
    )
    gain_one, shift_one, gain_two, shift_two = norms[0], norms[1], norms[2], norms[3]
    w_kv = gather_sq(jnp.concatenate([w_key, w_value], axis=1), 0, False)
    w_qs = gather_sq(jnp.concatenate([w_query, w_swish], axis=1), 0, True)
    out_rows = gather_sq(w_out, 1, False)
    down_rows = gather_sq(w_down, 1, True)
    gate_cols = gather_sq(w_gate, 0, False)
    up_cols = gather_sq(w_up, 0, True)

    normed = layer_norm(x_low.astype(wide), gain_one, shift_one).astype(low)
    kv = project(normed, w_kv)
    key_low = heads_of((kv[:, :query_width] * key_scale).astype(low), KD)
    value_low = heads_of(kv[:, query_width:].astype(low), VD)
    log_rate = log_decay(head_index * local_heads, local_heads)
    position = jnp.arange(length).astype(wide)
    reach = jnp.exp(log_rate[:, None] * (position + 1.0))
    tail = jnp.exp(log_rate[:, None] * (length - 1.0 - position))
    state = jnp.einsum(
        "hjd,hje->hde",
        (key_low.astype(wide) * tail[:, :, None]).astype(low),
        value_low,
        preferred_element_type=wide,
    )
    incoming = carried_from(state, log_rate, length, False)
    qs = project(normed, w_qs)
    query_low = heads_of(qs[:, :query_width].astype(low), KD)
    swish_pre = qs[:, query_width:]
    retained, mixing, decay = retain_forward(query_low, key_low, value_low, incoming, log_rate)
    grouped = rows_of(group_norm(retained).astype(low)).astype(wide)
    gated_low = swish_gate(grouped, swish_pre).astype(low)

    def out_part(start):
        return project(lax.dynamic_slice_in_dim(gated_low, start, own_rows, 0), out_rows)

    hidden = x_own.astype(wide) + scatter_head(out_part, own_rows)
    second_own = layer_norm(hidden, gain_two, shift_two).astype(low)
    second = gather_head(second_own)
    cot = gather_head(cot_own)
    gate_pre = project(second, gate_cols)
    up_pre = project(second, up_cols)
    inner_low = gelu_gate(gate_pre, up_pre).astype(low)

    def down_part(start):
        return project(lax.dynamic_slice_in_dim(inner_low, start, own_rows, 0), down_rows)

    grad_inner = back_project(cot, down_rows)
    _, gelu_back = jax.vjp(gelu_gate, gate_pre, up_pre)
    gate_grad, up_grad = gelu_back(grad_inner)
    gate_low = gate_grad.astype(low)
    up_low = up_grad.astype(low)

    def second_part(start):
        return back_project(
            lax.dynamic_slice_in_dim(gate_low, start, own_rows, 0), gate_cols
        ) + back_project(lax.dynamic_slice_in_dim(up_low, start, own_rows, 0), up_cols)

    second_grad = scatter_head(second_part, own_rows)
    _, second_back = jax.vjp(layer_norm, hidden, gain_two, shift_two)
    hidden_part, gain_two_part, shift_two_part = second_back(second_grad)
    grad_hidden = cot_own.astype(wide) + hidden_part
    branch_low = gather_head(grad_hidden.astype(low))
    result = (hidden + scatter_head(down_part, own_rows)).astype(low)

    gated_grad = back_project(branch_low, out_rows)
    _, swish_back = jax.vjp(swish_gate, grouped, swish_pre)
    grouped_grad, swish_grad = swish_back(gated_grad)
    swish_low = swish_grad.astype(low)
    grouped_grad = heads_of(grouped_grad.astype(low).astype(wide), VD)
    _, group_back = jax.vjp(group_norm, retained)
    retained_grad = group_back(grouped_grad)[0].astype(low)

    crossed = jnp.einsum(
        "hid,hie->hde",
        (query_low.astype(wide) * reach[:, :, None]).astype(low),
        retained_grad,
        preferred_element_type=wide,
    )
    returned = carried_from(crossed, log_rate, length, True).astype(low)
    mixing_grad = jnp.einsum("hie,hje->hij", retained_grad, value_low, preferred_element_type=wide)
    scores_grad = (mixing_grad * decay).astype(low)
    query_grad = jnp.einsum("hij,hjd->hid", scores_grad, key_low, preferred_element_type=wide)
    query_grad = query_grad + reach[:, :, None] * jnp.einsum(
        "hie,hde->hid", retained_grad, incoming.astype(low), preferred_element_type=wide
    )
    keys_grad = jnp.einsum("hij,hid->hjd", scores_grad, query_low, preferred_element_type=wide)
    keys_grad = keys_grad + tail[:, :, None] * jnp.einsum(
        "hje,hde->hjd", value_low, returned, preferred_element_type=wide
    )
    values_grad = jnp.einsum("hij,hie->hje", mixing, retained_grad, preferred_element_type=wide)
    values_grad = values_grad + tail[:, :, None] * jnp.einsum(
        "hjd,hde->hje", key_low, returned, preferred_element_type=wide
    )
    query_back = rows_of(query_grad.astype(low))
    key_back = rows_of(keys_grad.astype(low)) * key_scale
    value_back = rows_of(values_grad.astype(low))
    kv_back = jnp.concatenate([key_back.astype(low), value_back], axis=1)
    qs_back = jnp.concatenate([query_back, swish_low], axis=1)

    def normed_part(start):
        return back_project(
            lax.dynamic_slice_in_dim(kv_back, start, own_rows, 0), w_kv
        ) + back_project(lax.dynamic_slice_in_dim(qs_back, start, own_rows, 0), w_qs)

    normed_grad = scatter_head(normed_part, own_rows)
    _, first_back = jax.vjp(layer_norm, x_own.astype(wide), gain_one, shift_one)
    input_part, gain_one_part, shift_one_part = first_back(normed_grad)
    grad_in = grad_hidden + input_part

    half = x_own.shape[1] // 2

    def half_of(values, part):
        return lax.slice_in_dim(values, part * half, (part + 1) * half, axis=1)

    grad_down = scatter_sq(lambda p: outer_sum(inner_low, half_of(cot, p)), 1, True)
    grad_gate = scatter_sq(lambda p: outer_sum(half_of(second, p), gate_low), 0, False)
    grad_up = scatter_sq(lambda p: outer_sum(half_of(second, p), up_low), 0, True)
    grad_out = scatter_sq(lambda p: outer_sum(gated_low, half_of(branch_low, p)), 1, False)
    grad_kv = scatter_sq(lambda p: outer_sum(half_of(normed, p), kv_back), 0, False)
    grad_qs = scatter_sq(lambda p: outer_sum(half_of(normed, p), qs_back), 0, True)

    second_norm = sum_all(true_order(jnp.stack([gain_two_part, shift_two_part])))
    second_norm = lax.dynamic_slice_in_dim(
        second_norm, sq_index * norm2_gain.shape[0], norm2_gain.shape[0], 1
    )
    first_norm = sum_all(true_order(jnp.stack([gain_one_part, shift_one_part])))
    piece = first_norm.shape[1] // (count_sq * count_head)
    first_norm = lax.dynamic_slice_in_dim(
        first_norm, (head_index * count_sq + sq_index) * piece, piece, 1
    )
    return (
        true_order(result),
        true_order(grad_in),
        first_norm[0],
        first_norm[1],
        grad_qs[:, :query_width],
        grad_kv[:, :query_width],
        grad_kv[:, query_width:],
        grad_qs[:, query_width:],
        grad_out,
        second_norm[0],
        second_norm[1],
        grad_gate,
        grad_up,
        grad_down,
    )


def solution(mesh):
    return jax.shard_map(
        shards,
        mesh=mesh,
        in_specs=(
            P(("sq", "head"), None),
            P("sq"),
            P("sq"),
            P("sq", "head"),
            P("sq", "head"),
            P("sq", "head"),
            P("sq", "head"),
            P("head", "sq"),
            P("sq"),
            P("sq"),
            P("sq", "head"),
            P("sq", "head"),
            P("head", "sq"),
            P(("sq", "head"), None),
        ),
        out_specs=(
            P(("sq", "head"), None),
            P(("sq", "head"), None),
            P(("head", "sq")),
            P(("head", "sq")),
            P("sq", "head"),
            P("sq", "head"),
            P("sq", "head"),
            P("sq", "head"),
            P("head", "sq"),
            P("sq"),
            P("sq"),
            P("sq", "head"),
            P("sq", "head"),
            P("head", "sq"),
        ),
        check_vma=False,
    )
```

time: 1530 us -> 937 us (0.61)
  waiting for transfers between devices: 1030 us -> 479 us
  local copies, waits for them, and re-layouts: 15.1 us -> 106 us
  blocking collectives: 87.6 us -> 0 us
  starting transfers between devices: 2.54 us -> 66.9 us
  matrix products: 270 us -> 208 us
  other arithmetic: 96.9 us -> 67.5 us
    ppermute x0 -> x88, waiting for transfers between devices: none -> 479 us  [the longest x24 337 us: ring_step(): lax.ppermute(value, 'head', [(i, (i + 1) % count) for i in range(count)])]
    reduce_scatter x10 -> x0, waiting for transfers between devices: 368 us -> none  [the longest x1 77.3 us: shards(): lax.psum_scatter(project(inner_low, down_rows).astype(jnp.bfloat16), 'hea...]
    all_gather x12 -> x0, waiting for transfers between devices: 363 us -> none  [the longest x1 72.4 us: shards(): lax.all_gather(cotangent, 'head', axis=0, tiled=True)]
    psum x2 -> x0, waiting for transfers between devices: 291 us -> none  [the longest x1 155 us: shards(): lax.psum(hidden_part.astype(jnp.bfloat16), 'head').astype(jnp.float32)]
    ppermute x0 -> x88, starting transfers between devices: none -> 66.9 us  [the longest x54 51.1 us: flip(): return lax.ppermute(value, 'sq', [(i, i ^ mask) for i in range(count)])]
    all_gather x5 -> x0, blocking collectives: 44.9 us -> none  [the longest x1 10.3 us: shards(): lax.all_gather(norm1_bias, 'sq', axis=0, tiled=True)]
    unnamed x126 -> x267, local copies, waits for them, and re-layouts: 14.6 us -> 50.4 us
    unnamed x2 -> x0, blocking collectives: 34.4 us -> none
  transfers between devices with their start and end apart: 24 -> 88, of which waited for: 20 -> 44; matrix products, arithmetic and copies ran while one was open for 19% -> 31% of each run, Pallas kernels for 0% -> 0%
where the time goes in v1:
time: 937 us; the launch traced here: 931 us
  waiting for transfers between devices  479 us (51%)
  matrix products  208 us (22%)
  local copies, waits for them, and re-layouts  106 us (11%)
  other arithmetic  67.5 us (7%)
  starting transfers between devices  66.9 us (7%)
    ppermute x24, waiting for transfers between devices, ring_step(): lax.ppermute(value, 'head', [(i, (i + 1) % count) for i in range(count)])  337 us
    ppermute x54, waiting for transfers between devices, flip(): return lax.ppermute(value, 'sq', [(i, i ^ mask) for i in range(count)])  104 us
    dot_general x18, matrix products, back_project(): lax.dot_general(gradient, weight, (((1,), (1,)), ((), ())), preferred_ele...  73.8 us
    dot_general x12, matrix products, project(): return jnp.dot(left_side, right_side, preferred_element_type=jnp.float32)  56.3 us
    dot_general x12, matrix products, outer_sum(): lax.dot_general(left_side, right_side, (((0,), (0,)), ((), ())), preferre...  52.4 us
    ppermute x54, starting transfers between devices, flip(): return lax.ppermute(value, 'sq', [(i, i ^ mask) for i in range(count)])  51.1 us
    unnamed x267, local copies, waits for them, and re-layouts  50.4 us
    ppermute x10, waiting for transfers between devices, sum_all(): lax.ppermute(values, axis, [(i, i ^ step) for i in range(count)])  39 us
  transfers between devices with their start and end apart: 88, of which 44 were waited for; matrix products, arithmetic and copies ran while one was open for 31% of the time, Pallas kernels for 0%

profile of v1, /device:TPU:0, one launch (start us, length us, event | category | flops | bytes accessed | tf_op | source)
XLA Modules:
  0.0 931.0 jit_solution(8728030036204453419)
XLA Ops:
  48.9 6.5 collective-permute-done.20
  60.9 11.4 %collective-permute-done.8 = bf16[256,1536]{1,0:T(8,128)(2,1)S(1)} collective-permute-done((bf16[256,1536]{1,0:T(8,128)(2,1)}, bf16[256,1536]{1,0:T(8,128)(2,1)S(1)}, u32[]{:S(2)}, u32[]{:S(2)}) %collective-permute-start.8) | collective-permute-done | bytes 786464 | tf_op jit(solution)/shard_map/ppermute | solution.py:29
  75.2 8.3 collective-permute-done.21
  85.1 14.5 %collective-permute-done.13 = bf16[256,1536]{1,0:T(8,128)(2,1)S(1)} collective-permute-done((bf16[256,1536]{1,0:T(8,128)(2,1)S(1)}, bf16[256,1536]{1,0:T(8,128)(2,1)S(1)}, u32[]{:S(2)}, u32[]{:S(2)}) %collective-permute-start.13) | collective-permute-done | bytes 786464 | tf_op jit(solution)/shard_map/ppermute | solution.py:29
  112.5 16.0 %collective-permute-done.2 = bf16[256,2048]{1,0:T(8,128)(2,1)S(1)} collective-permute-done((bf16[256,2048]{1,0:T(8,128)(2,1)S(1)}, bf16[256,2048]{1,0:T(8,128)(2,1)S(1)}, u32[]{:S(2)}, u32[]{:S(2)}) %collective-permute-start.2) | collective-permute-done | bytes 1048608 | tf_op jit(solution)/shard_map/ppermute | solution.py:100
  142.1 8.7 fusion.235
  166.0 9.4 %collective-permute-done.15 = bf16[1,2,256,512]{3,2,1,0:T(8,128)(2,1)S(1)} collective-permute-done((bf16[1,2,256,512]{3,2,1,0:T(8,128)(2,1)S(1)}, bf16[1,2,256,512]{3,2,1,0:T(8,128)(2,1)S(1)}, u32[]{:S(2)}, u32[]{:S(2)}) %collective-permute-start.15) | collective-permute-done | bytes 524320 | tf_op jit(solution)/shard_map/ppermute | solution.py:29
  179.7 5.3 constant_dynamic-update-slice_fusion.15
  189.3 9.1 fusion.234
  215.2 5.4 copy.65
  220.6 5.0 multiply_convert_fusion.5
  234.4 21.0 %collective-permute-done.23 = bf16[256,2048]{1,0:T(8,128)(2,1)} collective-permute-done((bf16[256,2048]{1,0:T(8,128)(2,1)}, bf16[256,2048]{1,0:T(8,128)(2,1)}, u32[]{:S(2)}, u32[]{:S(2)}) %collective-permute-start.23) | collective-permute-done | bytes 1048608 | tf_op jit(solution)/shard_map/ppermute | solution.py:100
  263.3 23.0 %collective-permute-done.24 = bf16[256,2048]{1,0:T(8,128)(2,1)S(1)} collective-permute-done((bf16[256,2048]{1,0:T(8,128)(2,1)S(1)}, bf16[256,2048]{1,0:T(8,128)(2,1)S(1)}, u32[]{:S(2)}, u32[]{:S(2)}) %collective-permute-start.24) | collective-permute-done | bytes 1048608 | tf_op jit(solution)/shard_map/ppermute | solution.py:100
  293.8 9.5 %collective-permute-done.39 = bf16[1024,256]{1,0:T(8,128)(2,1)} collective-permute-done((bf16[1024,256]{1,0:T(8,128)(2,1)}, bf16[1024,256]{1,0:T(8,128)(2,1)}, u32[]{:S(2)}, u32[]{:S(2)}) %collective-permute-start.39) | collective-permute-done | bytes 524320 | tf_op jit(solution)/shard_map/ppermute | solution.py:29
  306.4 11.4 %collective-permute-done.25 = bf16[256,2048]{1,0:T(8,128)(2,1)} collective-permute-done((bf16[256,2048]{1,0:T(8,128)(2,1)}, bf16[256,2048]{1,0:T(8,128)(2,1)}, u32[]{:S(2)}, u32[]{:S(2)}) %collective-permute-start.25) | collective-permute-done | bytes 1048608 | tf_op jit(solution)/shard_map/ppermute | solution.py:100
  322.6 15.2 %collective-permute-done.44 = bf16[256,2048]{1,0:T(8,128)(2,1)S(1)} collective-permute-done((bf16[256,2048]{1,0:T(8,128)(2,1)S(1)}, bf16[256,2048]{1,0:T(8,128)(2,1)S(1)}, u32[]{:S(2)}, u32[]{:S(2)}) %collective-permute-start.44) | collective-permute-done | bytes 1048608 | tf_op jit(solution)/shard_map/ppermute | solution.py:100
  354.1 11.6 %collective-permute-done.45 = bf16[256,2048]{1,0:T(8,128)(2,1)S(1)} collective-permute-done((bf16[256,2048]{1,0:T(8,128)(2,1)S(1)}, bf16[256,2048]{1,0:T(8,128)(2,1)S(1)}, u32[]{:S(2)}, u32[]{:S(2)}) %collective-permute-start.45) | collective-permute-done | bytes 1048608 | tf_op jit(solution)/shard_map/ppermute | solution.py:100
  366.0 22.2 %collective-permute-done.26 = bf16[256,2048]{1,0:T(8,128)(2,1)S(1)} collective-permute-done((bf16[256,2048]{1,0:T(8,128)(2,1)S(1)}, bf16[256,2048]{1,0:T(8,128)(2,1)S(1)}, u32[]{:S(2)}, u32[]{:S(2)}) %collective-permute-start.26) | collective-permute-done | bytes 1048608 | tf_op jit(solution)/shard_map/ppermute | solution.py:100
  392.8 17.8 %collective-permute-done.46 = bf16[256,2048]{1,0:T(8,128)(2,1)S(1)} collective-permute-done((bf16[256,2048]{1,0:T(8,128)(2,1)S(1)}, bf16[256,2048]{1,0:T(8,128)(2,1)S(1)}, u32[]{:S(2)}, u32[]{:S(2)}) %collective-permute-start.46) | collective-permute-done | bytes 1048608 | tf_op jit(solution)/shard_map/ppermute | solution.py:100
  410.8 19.0 %collective-permute-done.27 = bf16[256,2048]{1,0:T(8,128)(2,1)S(1)} collective-permute-done((bf16[256,2048]{1,0:T(8,128)(2,1)S(1)}, bf16[256,2048]{1,0:T(8,128)(2,1)S(1)}, u32[]{:S(2)}, u32[]{:S(2)}) %collective-permute-start.27) | collective-permute-done | bytes 1048608 | tf_op jit(solution)/shard_map/ppermute | solution.py:100
  430.0 8.5 fusion.237
  439.1 14.5 %collective-permute-done.28 = bf16[256,2048]{1,0:T(8,128)(2,1)S(1)} collective-permute-done((bf16[256,2048]{1,0:T(8,128)(2,1)S(1)}, bf16[256,2048]{1,0:T(8,128)(2,1)S(1)}, u32[]{:S(2)}, u32[]{:S(2)}) %collective-permute-start.28) | collective-permute-done | bytes 1048608 | tf_op jit(solution)/shard_map/ppermute | solution.py:100
  453.7 6.1 fusion.236
  459.8 11.2 %fusion.12 = (bf16[1024,1024]{1,0:T(8,128)(2,1)S(1)}, bf16[1024,1024]{1,0:T(8,128)(2,1)S(1)}, bf16[1024,1024]{1,0:T(8,128)(2,1)}) fusion(f32[1024,1024]{1,0:T(8,128)} %fusion.237, f32[1024,1024]{1,0:T(8,128)} %fusion.236, bf16[1024,2048]{1,0:T(8,128)(2,1)S(1)} %constant_dynamic-update-slice_fusion.89, ...), kind=kOutput, calls=%fused_computation.35 | convolution fusion | flops 4322230272 | bytes 23068672 | tf_op jit(solution)/shard_map/dot_general | solution.py:162
  493.1 18.7 %collective-permute-done.47 = bf16[256,2048]{1,0:T(8,128)(2,1)S(1)} collective-permute-done((bf16[256,2048]{1,0:T(8,128)(2,1)S(1)}, bf16[256,2048]{1,0:T(8,128)(2,1)S(1)}, u32[]{:S(2)}, u32[]{:S(2)}) %collective-permute-start.47) | collective-permute-done | bytes 1048608 | tf_op jit(solution)/shard_map/ppermute | solution.py:100
  514.8 19.5 %collective-permute-done.41 = bf16[256,2048]{1,0:T(8,128)(2,1)S(1)} collective-permute-done((bf16[256,2048]{1,0:T(8,128)(2,1)S(1)}, bf16[256,2048]{1,0:T(8,128)(2,1)S(1)}, u32[]{:S(2)}, u32[]{:S(2)}) %collective-permute-start.41) | collective-permute-done | bytes 1048608 | tf_op jit(solution)/shard_map/ppermute | solution.py:100
  560.7 18.6 %collective-permute-done.42 = bf16[256,2048]{1,0:T(8,128)(2,1)} collective-permute-done((bf16[256,2048]{1,0:T(8,128)(2,1)}, bf16[256,2048]{1,0:T(8,128)(2,1)}, u32[]{:S(2)}, u32[]{:S(2)}) %collective-permute-start.42) | collective-permute-done | bytes 1048608 | tf_op jit(solution)/shard_map/ppermute | solution.py:100
  593.9 7.8 collective-permute-done.49
  606.5 17.7 %collective-permute-done.43 = bf16[256,2048]{1,0:T(8,128)(2,1)S(1)} collective-permute-done((bf16[256,2048]{1,0:T(8,128)(2,1)S(1)}, bf16[256,2048]{1,0:T(8,128)(2,1)S(1)}, u32[]{:S(2)}, u32[]{:S(2)}) %collective-permute-start.43) | collective-permute-done | bytes 1048608 | tf_op jit(solution)/shard_map/ppermute | solution.py:100
  628.3 18.1 %collective-permute-done.50 = bf16[256,2048]{1,0:T(8,128)(2,1)} collective-permute-done((bf16[256,2048]{1,0:T(8,128)(2,1)S(1)}, bf16[256,2048]{1,0:T(8,128)(2,1)}, u32[]{:S(2)}, u32[]{:S(2)}) %collective-permute-start.50) | collective-permute-done | bytes 1048608 | tf_op jit(solution)/shard_map/ppermute | solution.py:100
  650.4 23.1 %collective-permute-done.77 = f32[2,2048]{1,0:T(2,128)S(1)} collective-permute-done((f32[2,2048]{1,0:T(2,128)S(1)}, f32[2,2048]{1,0:T(2,128)S(1)}, u32[]{:S(2)}, u32[]{:S(2)}) %collective-permute-start.77) | collective-permute-done | bytes 16416 | tf_op jit(solution)/shard_map/ppermute | solution.py:133
  688.8 17.5 %collective-permute-done.52 = bf16[256,2048]{1,0:T(8,128)(2,1)S(1)} collective-permute-done((bf16[256,2048]{1,0:T(8,128)(2,1)}, bf16[256,2048]{1,0:T(8,128)(2,1)S(1)}, u32[]{:S(2)}, u32[]{:S(2)}) %collective-permute-start.52) | collective-permute-done | bytes 1048608 | tf_op jit(solution)/shard_map/ppermute | solution.py:100
  712.8 7.8 fusion.49
  720.5 5.3 copy.66
  748.5 7.2 convolution_convert_fusion.1
  755.8 5.1 collective-permute-done.55
  771.9 4.8 fusion.124
  793.7 5.5 add_convert_fusion.1
  804.8 5.5 convolution_convert_fusion
  815.3 16.6 %collective-permute-done.57 = bf16[256,2048]{1,0:T(8,128)(2,1)} collective-permute-done((bf16[256,2048]{1,0:T(8,128)(2,1)S(1)}, bf16[256,2048]{1,0:T(8,128)(2,1)}, u32[]{:S(2)}, u32[]{:S(2)}) %collective-permute-start.57) | collective-permute-done | bytes 1048608 | tf_op jit(solution)/shard_map/ppermute | solution.py:100
  831.9 5.0 fusion.35
  842.2 8.4 collective-permute-done.73
  851.9 11.5 %collective-permute-done.58 = bf16[256,2048]{1,0:T(8,128)(2,1)S(1)} collective-permute-done((bf16[256,2048]{1,0:T(8,128)(2,1)S(1)}, bf16[256,2048]{1,0:T(8,128)(2,1)S(1)}, u32[]{:S(2)}, u32[]{:S(2)}) %collective-permute-start.58) | collective-permute-done | bytes 1048608 | tf_op jit(solution)/shard_map/ppermute | solution.py:100
  863.4 4.7 fusion.34
  870.4 5.6 add_convert_fusion
  877.1 16.4 %collective-permute-done.59 = bf16[256,2048]{1,0:T(8,128)(2,1)S(1)} collective-permute-done((bf16[256,2048]{1,0:T(8,128)(2,1)S(1)}, bf16[256,2048]{1,0:T(8,128)(2,1)S(1)}, u32[]{:S(2)}, u32[]{:S(2)}) %collective-permute-start.59) | collective-permute-done | bytes 1048608 | tf_op jit(solution)/shard_map/ppermute | solution.py:100
  893.5 5.3 fusion.45
  903.4 7.5 collective-permute-done.69
  (605 shorter events, 374.0 us)
Async XLA Ops:
  3.3 30.9 %collective-permute-start.3 = (bf16[4,256]{1,0:T(4,128)(2,1)S(1)}, bf16[4,256]{1,0:T(4,128)(2,1)S(1)}, u32[]{:S(2)}, u32[]{:S(2)}) collective-permute-start(bf16[4,256]{1,0:T(4,128)(2,1)S(1)} %get-tuple-element.45), channel_id=1, source_target_pairs={{0,2},{1,3},{2,0},{3,1},{4,6},{5,7},{6,4},{7,5},{8,10},{9,11},{10,... | collective-permute-start | bytes 6152 | tf_op jit(solution)/shard_map/ppermute | solution.py:29
  6.3 29.5 %collective-permute-start.4 = (bf16[4,256]{1,0:T(4,128)(2,1)S(1)}, bf16[4,256]{1,0:T(4,128)(2,1)S(1)}, u32[]{:S(2)}, u32[]{:S(2)}) collective-permute-start(bf16[4,256]{1,0:T(4,128)(2,1)S(1)} %get-tuple-element.45), channel_id=1, source_target_pairs={{0,4},{1,5},{2,6},{3,7},{4,0},{5,1},{6,2},{7,3},{8,12},{9,13},{10,... | collective-permute-start | bytes 6152 | tf_op jit(solution)/shard_map/ppermute | solution.py:29
  11.8 45.2 %collective-permute-start.11 = (bf16[256,1536]{1,0:T(8,128)(2,1)}, bf16[256,1536]{1,0:T(8,128)(2,1)S(1)}, u32[]{:S(2)}, u32[]{:S(2)}) collective-permute-start(bf16[256,1536]{1,0:T(8,128)(2,1)} %get-tuple-element.59), channel_id=1, source_target_pairs={{0,2},{1,3},{2,0},{3,1},{4,6},{5,7},{6,4},{7,5},{8,10},{9,11},{10,... | collective-permute-start | bytes 2359304 | tf_op jit(solution)/shard_map/ppermute | solution.py:29
  12.3 60.5 %collective-permute-start.12 = (bf16[256,1536]{1,0:T(8,128)(2,1)}, bf16[256,1536]{1,0:T(8,128)(2,1)S(1)}, u32[]{:S(2)}, u32[]{:S(2)}) collective-permute-start(bf16[256,1536]{1,0:T(8,128)(2,1)} %get-tuple-element.59), channel_id=1, source_target_pairs={{0,4},{1,5},{2,6},{3,7},{4,0},{5,1},{6,2},{7,3},{8,12},{9,13},{10,... | collective-permute-start | bytes 2359304 | tf_op jit(solution)/shard_map/ppermute | solution.py:29
  20.6 37.8 %collective-permute-start = (bf16[256,2048]{1,0:T(8,128)(2,1)S(1)}, bf16[256,2048]{1,0:T(8,128)(2,1)}, u32[]{:S(2)}, u32[]{:S(2)}) collective-permute-start(bf16[256,2048]{1,0:T(8,128)(2,1)S(1)} %constant_dynamic-update-slice_fusion), channel_id=1, source_target_pairs={{0,8},{8,16},{16,24},{24,0},{1,9},{9,17},{17,25},{25,1},{2,10},{10... | collective-permute-start | bytes 3145736 | tf_op jit(solution)/shard_map/ppermute | solution.py:100
  56.9 42.6 %collective-permute-start.13 = (bf16[256,1536]{1,0:T(8,128)(2,1)S(1)}, bf16[256,1536]{1,0:T(8,128)(2,1)S(1)}, u32[]{:S(2)}, u32[]{:S(2)}) collective-permute-start(bf16[256,1536]{1,0:T(8,128)(2,1)S(1)} %collective-permute-done.11), channel_id=1, source_target_pairs={{0,4},{1,5},{2,6},{3,7},{4,0},{5,1},{6,2},{7,3},{8,12},{9,13},{10,... | collective-permute-start | bytes 2359304 | tf_op jit(solution)/shard_map/ppermute | solution.py:29
  58.3 42.6 %collective-permute-start.1 = (bf16[256,2048]{1,0:T(8,128)(2,1)}, bf16[256,2048]{1,0:T(8,128)(2,1)S(1)}, u32[]{:S(2)}, u32[]{:S(2)}) collective-permute-start(bf16[256,2048]{1,0:T(8,128)(2,1)} %collective-permute-done), channel_id=1, source_target_pairs={{0,8},{8,16},{16,24},{24,0},{1,9},{9,17},{17,25},{25,1},{2,10},{10... | collective-permute-start | bytes 3145736 | tf_op jit(solution)/shard_map/ppermute | solution.py:100
  72.3 32.8 %collective-permute-start.7 = (bf16[256,1536]{1,0:T(8,128)(2,1)}, bf16[256,1536]{1,0:T(8,128)(2,1)S(1)}, u32[]{:S(2)}, u32[]{:S(2)}) collective-permute-start(bf16[256,1536]{1,0:T(8,128)(2,1)} %get-tuple-element.57), channel_id=1, source_target_pairs={{0,2},{1,3},{2,0},{3,1},{4,6},{5,7},{6,4},{7,5},{8,10},{9,11},{10,... | collective-permute-start | bytes 2359304 | tf_op jit(solution)/shard_map/ppermute | solution.py:29
  72.8 34.5 %collective-permute-start.9 = (bf16[256,1536]{1,0:T(8,128)(2,1)S(1)}, bf16[256,1536]{1,0:T(8,128)(2,1)S(1)}, u32[]{:S(2)}, u32[]{:S(2)}) collective-permute-start(bf16[256,1536]{1,0:T(8,128)(2,1)S(1)} %collective-permute-done.8), channel_id=1, source_target_pairs={{0,2},{1,3},{2,0},{3,1},{4,6},{5,7},{6,4},{7,5},{8,10},{9,11},{10,... | collective-permute-start | bytes 2359304 | tf_op jit(solution)/shard_map/ppermute | solution.py:29
  85.1 92.7 %collective-permute-start.22 = (bf16[1024,1024]{1,0:T(8,128)(2,1)}, bf16[1024,1024]{1,0:T(8,128)(2,1)}, u32[]{:S(2)}, u32[]{:S(2)}) collective-permute-start(bf16[1024,1024]{1,0:T(8,128)(2,1)} %pad_maximum_fusion.5), channel_id=1, source_target_pairs={{0,1},{1,0},{2,3},{3,2},{4,5},{5,4},{6,7},{7,6},{8,9},{9,8},{10,11... | collective-permute-start | bytes 6291464 | tf_op jit(solution)/shard_map/ppermute | solution.py:29
  100.8 38.3 %collective-permute-start.14 = (bf16[1024,1536]{1,0:T(8,128)(2,1)S(1)}, bf16[1024,1536]{1,0:T(8,128)(2,1)S(1)}, u32[]{:S(2)}, u32[]{:S(2)}) collective-permute-start(bf16[1024,1536]{1,0:T(8,128)(2,1)S(1)} %pad_maximum_fusion.3), channel_id=1, source_target_pairs={{0,1},{1,0},{2,3},{3,2},{4,5},{5,4},{6,7},{7,6},{8,9},{9,8},{10,11... | collective-permute-start | bytes 9437192 | tf_op jit(solution)/shard_map/ppermute | solution.py:29
  110.5 69.2 %collective-permute-start.10 = (bf16[1024,1536]{1,0:T(8,128)(2,1)}, bf16[1024,1536]{1,0:T(8,128)(2,1)}, u32[]{:S(2)}, u32[]{:S(2)}) collective-permute-start(bf16[1024,1536]{1,0:T(8,128)(2,1)} %pad_maximum_fusion.2), channel_id=1, source_target_pairs={{0,1},{1,0},{2,3},{3,2},{4,5},{5,4},{6,7},{7,6},{8,9},{9,8},{10,11... | collective-permute-start | bytes 9437192 | tf_op jit(solution)/shard_map/ppermute | solution.py:29
  227.9 94.7 %collective-permute-start.34 = (bf16[256,1024]{1,0:T(8,128)(2,1)S(1)}, bf16[256,1024]{1,0:T(8,128)(2,1)}, u32[]{:S(2)}, u32[]{:S(2)}) collective-permute-start(bf16[256,1024]{1,0:T(8,128)(2,1)S(1)} %copy-done.56), channel_id=1, source_target_pairs={{0,4},{1,5},{2,6},{3,7},{4,0},{5,1},{6,2},{7,3},{8,12},{9,13},{10,... | collective-permute-start | bytes 1572872 | tf_op jit(solution)/shard_map/ppermute | solution.py:29
  229.5 109.4 %collective-permute-start.33 = (bf16[256,1024]{1,0:T(8,128)(2,1)S(1)}, bf16[256,1024]{1,0:T(8,128)(2,1)}, u32[]{:S(2)}, u32[]{:S(2)}) collective-permute-start(bf16[256,1024]{1,0:T(8,128)(2,1)S(1)} %copy-done.56), channel_id=1, source_target_pairs={{0,2},{1,3},{2,0},{3,1},{4,6},{5,7},{6,4},{7,5},{8,10},{9,11},{10,... | collective-permute-start | bytes 1572872 | tf_op jit(solution)/shard_map/ppermute | solution.py:29
  230.9 59.5 %collective-permute-start.38 = (bf16[1024,256]{1,0:T(8,128)(2,1)S(1)}, bf16[1024,256]{1,0:T(8,128)(2,1)}, u32[]{:S(2)}, u32[]{:S(2)}) collective-permute-start(bf16[1024,256]{1,0:T(8,128)(2,1)S(1)} %copy-done.55), channel_id=1, source_target_pairs={{0,4},{1,5},{2,6},{3,7},{4,0},{5,1},{6,2},{7,3},{8,12},{9,13},{10,... | collective-permute-start | bytes 1572872 | tf_op jit(solution)/shard_map/ppermute | solution.py:29
  231.5 62.3 %collective-permute-start.37 = (bf16[1024,256]{1,0:T(8,128)(2,1)S(1)}, bf16[1024,256]{1,0:T(8,128)(2,1)}, u32[]{:S(2)}, u32[]{:S(2)}) collective-permute-start(bf16[1024,256]{1,0:T(8,128)(2,1)S(1)} %copy-done.55), channel_id=1, source_target_pairs={{0,2},{1,3},{2,0},{3,1},{4,6},{5,7},{6,4},{7,5},{8,10},{9,11},{10,... | collective-permute-start | bytes 1572872 | tf_op jit(solution)/shard_map/ppermute | solution.py:29
  289.6 28.2 %collective-permute-start.25 = (bf16[256,2048]{1,0:T(8,128)(2,1)}, bf16[256,2048]{1,0:T(8,128)(2,1)}, u32[]{:S(2)}, u32[]{:S(2)}) collective-permute-start(bf16[256,2048]{1,0:T(8,128)(2,1)} %fusion.40), channel_id=1, source_target_pairs={{0,8},{8,16},{16,24},{24,0},{1,9},{9,17},{17,25},{25,1},{2,10},{10... | collective-permute-start | bytes 3145736 | tf_op jit(solution)/shard_map/ppermute | solution.py:100
  293.7 44.1 %collective-permute-start.44 = (bf16[256,2048]{1,0:T(8,128)(2,1)S(1)}, bf16[256,2048]{1,0:T(8,128)(2,1)S(1)}, u32[]{:S(2)}, u32[]{:S(2)}) collective-permute-start(bf16[256,2048]{1,0:T(8,128)(2,1)S(1)} %constant_dynamic-update-slice_fusion.57), channel_id=1, source_target_pairs={{0,8},{8,16},{16,24},{24,0},{1,9},{9,17},{17,25},{25,1},{2,10},{10... | collective-permute-start | bytes 3145736 | tf_op jit(solution)/shard_map/ppermute | solution.py:100
  303.3 37.6 %collective-permute-start.29 = (bf16[256,1024]{1,0:T(8,128)(2,1)S(1)}, bf16[256,1024]{1,0:T(8,128)(2,1)S(1)}, u32[]{:S(2)}, u32[]{:S(2)}) collective-permute-start(bf16[256,1024]{1,0:T(8,128)(2,1)S(1)} %copy-done.58), channel_id=1, source_target_pairs={{0,2},{1,3},{2,0},{3,1},{4,6},{5,7},{6,4},{7,5},{8,10},{9,11},{10,... | collective-permute-start | bytes 1572872 | tf_op jit(solution)/shard_map/ppermute | solution.py:29
  317.8 28.3 %collective-permute-start.30 = (bf16[256,1024]{1,0:T(8,128)(2,1)S(1)}, bf16[256,1024]{1,0:T(8,128)(2,1)S(1)}, u32[]{:S(2)}, u32[]{:S(2)}) collective-permute-start(bf16[256,1024]{1,0:T(8,128)(2,1)S(1)} %copy-done.58), channel_id=1, source_target_pairs={{0,4},{1,5},{2,6},{3,7},{4,0},{5,1},{6,2},{7,3},{8,12},{9,13},{10,... | collective-permute-start | bytes 1572872 | tf_op jit(solution)/shard_map/ppermute | solution.py:29
  322.6 68.7 %collective-permute-start.40 = (bf16[1024,1024]{1,0:T(8,128)(2,1)S(1)}, bf16[1024,1024]{1,0:T(8,128)(2,1)S(1)}, u32[]{:S(2)}, u32[]{:S(2)}) collective-permute-start(bf16[1024,1024]{1,0:T(8,128)(2,1)S(1)} %pad_maximum_fusion.8), channel_id=1, source_target_pairs={{0,1},{1,0},{2,3},{3,2},{4,5},{5,4},{6,7},{7,6},{8,9},{9,8},{10,11... | collective-permute-start | bytes 6291464 | tf_op jit(solution)/shard_map/ppermute | solution.py:29
  338.8 49.3 %collective-permute-start.26 = (bf16[256,2048]{1,0:T(8,128)(2,1)S(1)}, bf16[256,2048]{1,0:T(8,128)(2,1)S(1)}, u32[]{:S(2)}, u32[]{:S(2)}) collective-permute-start(bf16[256,2048]{1,0:T(8,128)(2,1)S(1)} %get-tuple-element.41), channel_id=1, source_target_pairs={{0,8},{8,16},{16,24},{24,0},{1,9},{9,17},{17,25},{25,1},{2,10},{10... | collective-permute-start | bytes 3145736 | tf_op jit(solution)/shard_map/ppermute | solution.py:100
  354.0 84.5 %collective-permute-start.36 = (bf16[1024,1024]{1,0:T(8,128)(2,1)S(1)}, bf16[1024,1024]{1,0:T(8,128)(2,1)S(1)}, u32[]{:S(2)}, u32[]{:S(2)}) collective-permute-start(bf16[1024,1024]{1,0:T(8,128)(2,1)S(1)} %pad_maximum_fusion.7), channel_id=1, source_target_pairs={{0,1},{1,0},{2,3},{3,2},{4,5},{5,4},{6,7},{7,6},{8,9},{9,8},{10,11... | collective-permute-start | bytes 6291464 | tf_op jit(solution)/shard_map/ppermute | solution.py:29
  365.7 44.9 %collective-permute-start.46 = (bf16[256,2048]{1,0:T(8,128)(2,1)S(1)}, bf16[256,2048]{1,0:T(8,128)(2,1)S(1)}, u32[]{:S(2)}, u32[]{:S(2)}) collective-permute-start(bf16[256,2048]{1,0:T(8,128)(2,1)S(1)} %collective-permute-done.45), channel_id=1, source_target_pairs={{0,8},{8,16},{16,24},{24,0},{1,9},{9,17},{17,25},{25,1},{2,10},{10... | collective-permute-start | bytes 3145736 | tf_op jit(solution)/shard_map/ppermute | solution.py:100
  365.9 72.8 %collective-permute-start.32 = (bf16[1024,1024]{1,0:T(8,128)(2,1)S(1)}, bf16[1024,1024]{1,0:T(8,128)(2,1)S(1)}, u32[]{:S(2)}, u32[]{:S(2)}) collective-permute-start(bf16[1024,1024]{1,0:T(8,128)(2,1)S(1)} %pad_maximum_fusion.6), channel_id=1, source_target_pairs={{0,1},{1,0},{2,3},{3,2},{4,5},{5,4},{6,7},{7,6},{8,9},{9,8},{10,11... | collective-permute-start | bytes 6291464 | tf_op jit(solution)/shard_map/ppermute | solution.py:29
  388.2 41.6 %collective-permute-start.27 = (bf16[256,2048]{1,0:T(8,128)(2,1)S(1)}, bf16[256,2048]{1,0:T(8,128)(2,1)S(1)}, u32[]{:S(2)}, u32[]{:S(2)}) collective-permute-start(bf16[256,2048]{1,0:T(8,128)(2,1)S(1)} %collective-permute-done.26), channel_id=1, source_target_pairs={{0,8},{8,16},{16,24},{24,0},{1,9},{9,17},{17,25},{25,1},{2,10},{10... | collective-permute-start | bytes 3145736 | tf_op jit(solution)/shard_map/ppermute | solution.py:100
  478.9 58.2 %collective-permute-start.85 = (bf16[1024,1024]{0,1:T(8,128)(2,1)S(1)}, bf16[1024,1024]{0,1:T(8,128)(2,1)}, u32[]{:S(2)}, u32[]{:S(2)}) collective-permute-start(bf16[1024,1024]{0,1:T(8,128)(2,1)S(1)} %fusion.68), channel_id=1, source_target_pairs={{0,1},{1,0},{2,3},{3,2},{4,5},{5,4},{6,7},{7,6},{8,9},{9,8},{10,11... | collective-permute-start | bytes 6291464 | tf_op jit(solution)/shard_map/ppermute | solution.py:29
  484.1 50.2 %collective-permute-start.41 = (bf16[256,2048]{1,0:T(8,128)(2,1)S(1)}, bf16[256,2048]{1,0:T(8,128)(2,1)S(1)}, u32[]{:S(2)}, u32[]{:S(2)}) collective-permute-start(bf16[256,2048]{1,0:T(8,128)(2,1)S(1)} %convolution_convert_fusion.2), channel_id=1, source_target_pairs={{0,8},{8,16},{16,24},{24,0},{1,9},{9,17},{17,25},{25,1},{2,10},{10... | collective-permute-start | bytes 3145736 | tf_op jit(solution)/shard_map/ppermute | solution.py:100
  489.9 52.8 %collective-permute-start.82 = (bf16[1024,1024]{1,0:T(8,128)(2,1)S(1)}, bf16[1024,1024]{1,0:T(8,128)(2,1)}, u32[]{:S(2)}, u32[]{:S(2)}) collective-permute-start(bf16[1024,1024]{1,0:T(8,128)(2,1)S(1)} %convolution_convert_fusion.4), channel_id=1, source_target_pairs={{0,1},{1,0},{2,3},{3,2},{4,5},{5,4},{6,7},{7,6},{8,9},{9,8},{10,11... | collective-permute-start | bytes 6291464 | tf_op jit(solution)/shard_map/ppermute | solution.py:29
  493.1 55.3 %collective-permute-start.79 = (bf16[1024,1024]{1,0:T(8,128)(2,1)}, bf16[1024,1024]{1,0:T(8,128)(2,1)}, u32[]{:S(2)}, u32[]{:S(2)}) collective-permute-start(bf16[1024,1024]{1,0:T(8,128)(2,1)} %convolution_convert_fusion.5), channel_id=1, source_target_pairs={{0,1},{1,0},{2,3},{3,2},{4,5},{5,4},{6,7},{7,6},{8,9},{9,8},{10,11... | collective-permute-start | bytes 6291464 | tf_op jit(solution)/shard_map/ppermute | solution.py:29
  514.8 42.0 %collective-permute-start.48 = (bf16[256,2048]{1,0:T(8,128)(2,1)S(1)}, bf16[256,2048]{1,0:T(8,128)(2,1)S(1)}, u32[]{:S(2)}, u32[]{:S(2)}) collective-permute-start(bf16[256,2048]{1,0:T(8,128)(2,1)S(1)} %fusion.37), channel_id=1, source_target_pairs={{0,8},{8,16},{16,24},{24,0},{1,9},{9,17},{17,25},{25,1},{2,10},{10... | collective-permute-start | bytes 3145736 | tf_op jit(solution)/shard_map/ppermute | solution.py:100
  536.6 42.8 %collective-permute-start.42 = (bf16[256,2048]{1,0:T(8,128)(2,1)}, bf16[256,2048]{1,0:T(8,128)(2,1)}, u32[]{:S(2)}, u32[]{:S(2)}) collective-permute-start(bf16[256,2048]{1,0:T(8,128)(2,1)} %fusion.43), channel_id=1, source_target_pairs={{0,8},{8,16},{16,24},{24,0},{1,9},{9,17},{17,25},{25,1},{2,10},{10... | collective-permute-start | bytes 3145736 | tf_op jit(solution)/shard_map/ppermute | solution.py:100
  541.3 41.0 %collective-permute-start.86 = (bf16[1024,512]{0,1:T(8,128)(2,1)S(1)}, bf16[1024,512]{0,1:T(8,128)(2,1)S(1)}, u32[]{:S(2)}, u32[]{:S(2)}) collective-permute-start(bf16[1024,512]{0,1:T(8,128)(2,1)S(1)} %pad_maximum_fusion.20), channel_id=1, source_target_pairs={{0,2},{1,3},{2,0},{3,1},{4,6},{5,7},{6,4},{7,5},{8,10},{9,11},{10,... | collective-permute-start | bytes 3145736 | tf_op jit(solution)/shard_map/ppermute | solution.py:29
  547.0 41.2 %collective-permute-start.83 = (bf16[512,1024]{1,0:T(8,128)(2,1)S(1)}, bf16[512,1024]{1,0:T(8,128)(2,1)S(1)}, u32[]{:S(2)}, u32[]{:S(2)}) collective-permute-start(bf16[512,1024]{1,0:T(8,128)(2,1)S(1)} %pad_maximum_fusion.19), channel_id=1, source_target_pairs={{0,2},{1,3},{2,0},{3,1},{4,6},{5,7},{6,4},{7,5},{8,10},{9,11},{10,... | collective-permute-start | bytes 3145736 | tf_op jit(solution)/shard_map/ppermute | solution.py:29
  552.5 38.4 %collective-permute-start.80 = (bf16[512,1024]{1,0:T(8,128)(2,1)S(1)}, bf16[512,1024]{1,0:T(8,128)(2,1)S(1)}, u32[]{:S(2)}, u32[]{:S(2)}) collective-permute-start(bf16[512,1024]{1,0:T(8,128)(2,1)S(1)} %concatenate.137), channel_id=1, source_target_pairs={{0,4},{1,5},{2,6},{3,7},{4,0},{5,1},{6,2},{7,3},{8,12},{9,13},{10,... | collective-permute-start | bytes 3145736 | tf_op jit(solution)/shard_map/ppermute | solution.py:29
  560.7 41.0 %collective-permute-start.49 = (bf16[256,2048]{1,0:T(8,128)(2,1)}, bf16[256,2048]{1,0:T(8,128)(2,1)S(1)}, u32[]{:S(2)}, u32[]{:S(2)}) collective-permute-start(bf16[256,2048]{1,0:T(8,128)(2,1)} %fusion.38), channel_id=1, source_target_pairs={{0,8},{8,16},{16,24},{24,0},{1,9},{9,17},{17,25},{25,1},{2,10},{10... | collective-permute-start | bytes 3145736 | tf_op jit(solution)/shard_map/ppermute | solution.py:100
  582.1 42.1 %collective-permute-start.43 = (bf16[256,2048]{1,0:T(8,128)(2,1)S(1)}, bf16[256,2048]{1,0:T(8,128)(2,1)S(1)}, u32[]{:S(2)}, u32[]{:S(2)}) collective-permute-start(bf16[256,2048]{1,0:T(8,128)(2,1)S(1)} %fusion.42), channel_id=1, source_target_pairs={{0,8},{8,16},{16,24},{24,0},{1,9},{9,17},{17,25},{25,1},{2,10},{10... | collective-permute-start | bytes 3145736 | tf_op jit(solution)/shard_map/ppermute | solution.py:100
  582.7 96.1 %collective-permute-start.87 = (bf16[1024,256]{0,1:T(8,128)(2,1)S(1)}, bf16[1024,256]{0,1:T(8,128)(2,1)S(1)}, u32[]{:S(2)}, u32[]{:S(2)}) collective-permute-start(bf16[1024,256]{0,1:T(8,128)(2,1)S(1)} %fusion.93), channel_id=1, source_target_pairs={{0,4},{1,5},{2,6},{3,7},{4,0},{5,1},{6,2},{7,3},{8,12},{9,13},{10,... | collective-permute-start | bytes 1572872 | tf_op jit(solution)/shard_map/ppermute | solution.py:29
  589.6 90.8 %collective-permute-start.84 = (bf16[256,1024]{1,0:T(8,128)(2,1)}, bf16[256,1024]{1,0:T(8,128)(2,1)}, u32[]{:S(2)}, u32[]{:S(2)}) collective-permute-start(bf16[256,1024]{1,0:T(8,128)(2,1)} %fusion.95), channel_id=1, source_target_pairs={{0,4},{1,5},{2,6},{3,7},{4,0},{5,1},{6,2},{7,3},{8,12},{9,13},{10,... | collective-permute-start | bytes 1572872 | tf_op jit(solution)/shard_map/ppermute | solution.py:29
  592.4 90.5 %collective-permute-start.81 = (bf16[256,1024]{1,0:T(8,128)(2,1)}, bf16[256,1024]{1,0:T(8,128)(2,1)}, u32[]{:S(2)}, u32[]{:S(2)}) collective-permute-start(bf16[256,1024]{1,0:T(8,128)(2,1)} %fusion.97), channel_id=1, source_target_pairs={{0,2},{1,3},{2,0},{3,1},{4,6},{5,7},{6,4},{7,5},{8,10},{9,11},{10,... | collective-permute-start | bytes 1572872 | tf_op jit(solution)/shard_map/ppermute | solution.py:29
  605.8 40.5 %collective-permute-start.50 = (bf16[256,2048]{1,0:T(8,128)(2,1)S(1)}, bf16[256,2048]{1,0:T(8,128)(2,1)}, u32[]{:S(2)}, u32[]{:S(2)}) collective-permute-start(bf16[256,2048]{1,0:T(8,128)(2,1)S(1)} %get-tuple-element.37), channel_id=1, source_target_pairs={{0,8},{8,16},{16,24},{24,0},{1,9},{9,17},{17,25},{25,1},{2,10},{10... | collective-permute-start | bytes 3145736 | tf_op jit(solution)/shard_map/ppermute | solution.py:100
  646.4 34.0 %collective-permute-start.51 = (bf16[256,2048]{1,0:T(8,128)(2,1)}, bf16[256,2048]{1,0:T(8,128)(2,1)}, u32[]{:S(2)}, u32[]{:S(2)}) collective-permute-start(bf16[256,2048]{1,0:T(8,128)(2,1)} %collective-permute-done.50), channel_id=1, source_target_pairs={{0,8},{8,16},{16,24},{24,0},{1,9},{9,17},{17,25},{25,1},{2,10},{10... | collective-permute-start | bytes 3145736 | tf_op jit(solution)/shard_map/ppermute | solution.py:100
  742.4 34.3 %collective-permute-start.71 = (bf16[1024,1024]{1,0:T(8,128)(2,1)}, bf16[1024,1024]{1,0:T(8,128)(2,1)}, u32[]{:S(2)}, u32[]{:S(2)}) collective-permute-start(bf16[1024,1024]{1,0:T(8,128)(2,1)} %fusion.65), channel_id=1, source_target_pairs={{0,1},{1,0},{2,3},{3,2},{4,5},{5,4},{6,7},{7,6},{8,9},{9,8},{10,11... | collective-permute-start | bytes 6291464 | tf_op jit(solution)/shard_map/ppermute | solution.py:29
  755.8 37.9 %collective-permute-start.65 = (bf16[1024,1536]{1,0:T(8,128)(2,1)}, bf16[1024,1536]{1,0:T(8,128)(2,1)}, u32[]{:S(2)}, u32[]{:S(2)}) collective-permute-start(bf16[1024,1536]{1,0:T(8,128)(2,1)} %convolution_convert_fusion.1), channel_id=1, source_target_pairs={{0,1},{1,0},{2,3},{3,2},{4,5},{5,4},{6,7},{7,6},{8,9},{9,8},{10,11... | collective-permute-start | bytes 9437192 | tf_op jit(solution)/shard_map/ppermute | solution.py:29
  781.9 33.1 %collective-permute-start.72 = (bf16[1024,512]{1,0:T(8,128)(2,1)}, bf16[1024,512]{1,0:T(8,128)(2,1)S(1)}, u32[]{:S(2)}, u32[]{:S(2)}) collective-permute-start(bf16[1024,512]{1,0:T(8,128)(2,1)} %concatenate.136), channel_id=1, source_target_pairs={{0,4},{1,5},{2,6},{3,7},{4,0},{5,1},{6,2},{7,3},{8,12},{9,13},{10,... | collective-permute-start | bytes 3145736 | tf_op jit(solution)/shard_map/ppermute | solution.py:29
  799.4 39.6 %collective-permute-start.66 = (bf16[512,1536]{1,0:T(8,128)(2,1)S(1)}, bf16[512,1536]{1,0:T(8,128)(2,1)}, u32[]{:S(2)}, u32[]{:S(2)}) collective-permute-start(bf16[512,1536]{1,0:T(8,128)(2,1)S(1)} %pad_maximum_fusion.18), channel_id=1, source_target_pairs={{0,2},{1,3},{2,0},{3,1},{4,6},{5,7},{6,4},{7,5},{8,10},{9,11},{10,... | collective-permute-start | bytes 4718600 | tf_op jit(solution)/shard_map/ppermute | solution.py:29
  810.2 60.1 %collective-permute-start.68 = (bf16[1024,1536]{1,0:T(8,128)(2,1)}, bf16[1024,1536]{1,0:T(8,128)(2,1)}, u32[]{:S(2)}, u32[]{:S(2)}) collective-permute-start(bf16[1024,1536]{1,0:T(8,128)(2,1)} %convolution_convert_fusion), channel_id=1, source_target_pairs={{0,1},{1,0},{2,3},{3,2},{4,5},{5,4},{6,7},{7,6},{8,9},{9,8},{10,11... | collective-permute-start | bytes 9437192 | tf_op jit(solution)/shard_map/ppermute | solution.py:29
  876.2 34.8 %collective-permute-start.69 = (bf16[512,1536]{1,0:T(8,128)(2,1)S(1)}, bf16[512,1536]{1,0:T(8,128)(2,1)S(1)}, u32[]{:S(2)}, u32[]{:S(2)}) collective-permute-start(bf16[512,1536]{1,0:T(8,128)(2,1)S(1)} %concatenate.135), channel_id=1, source_target_pairs={{0,4},{1,5},{2,6},{3,7},{4,0},{5,1},{6,2},{7,3},{8,12},{9,13},{10,... | collective-permute-start | bytes 4718600 | tf_op jit(solution)/shard_map/ppermute | solution.py:29
  (146 other events, 2873.2 us)
